TPU v7x, 512 devices: a whole 4x4x16 slice. The times are simulated.
512 devices in a mesh: leaf: 32 (over x, y, core), top: 16 (over z).
Axes of the slice: x: 4, y: 4, z: 16, core: 2. Of those that a mesh axis runs over, the one named last changes fastest.
Arguments:
- features: bfloat16 [64, 524288], P(None, ('top', 'leaf')), may hold values from -6 to 6
- lengthscale: float32 [64], replicated, may hold values from 3 to 8
- signal_var: float32 [1], replicated, may hold values from 0.5 to 2
- noise_var: float32 [1], replicated, may hold values from 0.5 to 2
- factors: bfloat16 [8, 524288, 128], P(None, ('top', 'leaf')), may hold values from -3.75 to 4.75
- gains: float32 [8, 128], replicated, may hold values from 6.042172e-06 to 0.00068359375, as said below
- solution: float32 [64, 524288], P(None, ('top', 'leaf')), may hold values from -6 to 6
- residual: float32 [64, 524288], P(None, ('top', 'leaf')), may hold values from -41 to 41
- direction: float32 [64, 524288], P(None, ('top', 'leaf')), may hold values from -41 to 41
Outputs:
- new_solution: float32 [64, 524288], P(None, ('top', 'leaf'))
- new_residual: float32 [64, 524288], P(None, ('top', 'leaf'))
- new_direction: float32 [64, 524288], P(None, ('top', 'leaf'))
Inputs may be any that keep to these rules, and one draw needn't show every extreme that they name: gains are positive; the gains of level k lie within a factor of 10 of 0.35 / sqrt(128 * 1024 * 2^k).
All inputs are finite; a program needn't handle non-finite values.
Results may differ from a plain program's by a relative error of at most 0.001.
Values may be sent and summed in bfloat16 or wider, within the bound.
No kernel may reach another device: no remote copies, remote signals or barrier semaphores. Data moves between devices by JAX's collectives and lax.ppermute only.
A program may use at most 64 MiB of HBM per device.

v0:
```python
import jax
import jax.numpy as jnp
from jax import lax
from jax.sharding import PartitionSpec as P


def partner(block, axis, bit):
    count = lax.axis_size(axis)
    route = []
    for low in range(count):
        high = low | 1 << bit
        if high != low and high < count:
            route += [(low, high), (high, low)]
    return lax.ppermute(block, axis, route)


def shortened(array):
    return jax.tree.map(lambda a: a.astype(jnp.bfloat16) if a.dtype == jnp.float32 else a, array)


def leaf_part(own_scaled, own_sq, other_scaled, other_sq, other_dir, signal):
    inner = lax.dot_general(
        own_scaled,
        other_scaled,
        (((0,), (0,)), ((), ())),
        precision=lax.Precision.HIGHEST,
        preferred_element_type=jnp.float32,
    )
    kernel = signal * jnp.exp(-0.5 * (own_sq[:, None] + other_sq[None, :] - 2.0 * inner))
    return lax.dot_general(
        other_dir,
        kernel,
        (((1,), (1,)), ((), ())),
        precision=lax.Precision.HIGHEST,
        preferred_element_type=jnp.float32,
    )


def combine_bit(projection, received, lowest):
    if lowest < 0:
        return projection + received
    return jnp.concatenate(
        [projection[:lowest], received[:1], projection[lowest + 1 :] + received[1:]], axis=0
    )


def local(
    features, lengthscale, signal_var, noise_var, factors, gains, solution, residual, direction
):
    signal = signal_var[0]
    scaled = features.astype(jnp.float32) / lengthscale[:, None]
    own_sq = jnp.sum(scaled * scaled, axis=0)
    partner_feat = partner(features, "leaf", 0)
    partner_dir = partner(direction, "leaf", 0)
    other_scaled = partner_feat.astype(jnp.float32) / lengthscale[:, None]
    other_sq = jnp.sum(other_scaled * other_scaled, axis=0)
    direction_low = direction.astype(jnp.bfloat16)
    projection = jnp.einsum(
        "cp,lpr->lcr", direction_low, factors, preferred_element_type=jnp.float32
    )
    image = noise_var[0] * direction
    image = image + leaf_part(scaled, own_sq, scaled, own_sq, direction, signal)
    image = image + leaf_part(scaled, own_sq, other_scaled, other_sq, partner_dir, signal)
    leaf_bits = lax.axis_size("leaf").bit_length() - 1
    top_bits = lax.axis_size("top").bit_length() - 1
    for b in range(leaf_bits):
        lowest = b - 1
        received = partner(shortened(projection[max(lowest, 0) :]), "leaf", b)
        projection = combine_bit(projection, received, lowest)
    for t in range(top_bits):
        lowest = leaf_bits + t - 1
        received = partner(shortened(projection[lowest:]), "top", t)
        projection = combine_bit(projection, received, lowest)
    weighted = (gains[:, None, :] * projection).astype(jnp.bfloat16)
    image = image + jnp.einsum("lcr,lpr->cp", weighted, factors, preferred_element_type=jnp.float32)
    norm_now = lax.psum(jnp.sum(residual * residual, axis=1), ("leaf", "top"))
    curvature = lax.psum(jnp.sum(direction * image, axis=1), ("leaf", "top"))
    step_size = norm_now / curvature
    new_solution = solution + step_size[:, None] * direction
    new_residual = residual - step_size[:, None] * image
    norm_next = lax.psum(jnp.sum(new_residual * new_residual, axis=1), ("leaf", "top"))
    new_direction = new_residual + (norm_next / norm_now)[:, None] * direction
    return (new_solution, new_residual, new_direction)


def solution(mesh):
    return jax.shard_map(
        local,
        mesh=mesh,
        in_specs=(
            P(None, ("top", "leaf")),
            P(),
            P(),
            P(),
            P(None, ("top", "leaf"), None),
            P(),
            P(None, ("top", "leaf")),
            P(None, ("top", "leaf")),
            P(None, ("top", "leaf")),
        ),
        out_specs=(P(None, ("top", "leaf")), P(None, ("top", "leaf")), P(None, ("top", "leaf"))),
        check_vma=False,
    )
```

profile of v0, /device:TPU:1, one launch (start us, length us, event | category | flops | bytes accessed | tf_op | source)
XLA Modules:
  0.0 303.0 jit_solution(7086302006305492159)
XLA Ops:
  0.6 0.0 copy-start
  0.7 0.0 copy-start.1
  0.7 9.0 %collective-permute-start.1 = (f32[64,1024]{1,0:T(8,128)}, f32[64,1024]{1,0:T(8,128)S(1)}, u32[]{:S(2)}, u32[]{:S(2)}) collective-permute-start(f32[64,1024]{1,0:T(8,128)} %param.17), channel_id=1, source_target_pairs={{0,16},{16,0},{32,48},{48,32},{64,80},{80,64},{96,112},{112,96},{1... | collective-permute-start | bytes 786440 | tf_op jit(solution)/shard_map/ppermute | solution.py:14
  9.8 1.4 fusion.57
  11.2 1.9 collective-permute-start.2
  13.1 2.4 collective-permute-start
  15.5 4.7 %fusion.49 = f32[1024,1024]{1,0:T(8,128)S(1)} fusion(bf16[64,1024]{1,0:T(8,128)(2,1)} %param.9, f32[64]{0:T(128)} %param.10), kind=kOutput, calls=%fused_computation.68 | convolution fusion | flops 805437440 | bytes 4325632 | tf_op jit(solution)/shard_map/dot_general | solution.py:22
  21.6 0.1 multiply_reduce_fusion.4
  21.8 2.1 collective-permute-start.3
  23.9 0.2 multiply_reduce_fusion.2
  24.1 5.2 %fusion.36 = f32[64,1024]{1,0:T(8,128)S(1)} fusion(f32[64,1024]{1,0:T(8,128)S(1)} %copy-done.4, f32[1024,1024]{1,0:T(8,128)S(1)} %fusion.49, f32[1024]{0:T(1024)S(1)} %get-tuple-element.4, f32[]{:T(128)} %bitcast.25, f32[]{:T(128)} %bitcast.27), kind=kOutput, calls=%fused_computation.30 | convolution fusion | flops 810680320 | bytes 4722696 | tf_op jit(solution)/shard_map/dot_general | solution.py:30
  29.3 3.7 %fusion.39 = f32[1024,1024]{1,0:T(8,128)S(1)} fusion(bf16[64,1024]{1,0:T(8,128)(2,1)S(1)} %collective-permute-done, f32[64]{0:T(128)S(1)} %copy-done.6, bf16[64,1024]{1,0:T(8,128)(2,1)S(1)} %copy-done.1), kind=kOutput, calls=%fused_computation.45 | convolution fusion | flops 805568512 | bytes 4456704 | tf_op jit(solution)/shard_map/dot_general | solution.py:22
  33.0 1.9 collective-permute-start.4
  34.9 6.2 %collective-permute-done.4 = bf16[7,64,128]{2,1,0:T(8,128)(2,1)S(1)} collective-permute-done((bf16[7,64,128]{2,1,0:T(8,128)(2,1)S(1)}, bf16[7,64,128]{2,1,0:T(8,128)(2,1)S(1)}, u32[]{:S(2)}, u32[]{:S(2)}) %collective-permute-start.4) | collective-permute-done | bytes 114720 | tf_op jit(solution)/shard_map/ppermute | solution.py:14
  41.2 1.9 collective-permute-start.5
  43.1 3.4 %collective-permute-done.5 = bf16[6,64,128]{2,1,0:T(8,128)(2,1)S(1)} collective-permute-done((bf16[6,64,128]{2,1,0:T(8,128)(2,1)S(1)}, bf16[6,64,128]{2,1,0:T(8,128)(2,1)S(1)}, u32[]{:S(2)}, u32[]{:S(2)}) %collective-permute-start.5) | collective-permute-done | bytes 98336 | tf_op jit(solution)/shard_map/ppermute | solution.py:14
  46.6 1.9 collective-permute-start.6
  48.5 4.7 %collective-permute-done.6 = bf16[5,64,128]{2,1,0:T(8,128)(2,1)S(1)} collective-permute-done((bf16[5,64,128]{2,1,0:T(8,128)(2,1)S(1)}, bf16[5,64,128]{2,1,0:T(8,128)(2,1)S(1)}, u32[]{:S(2)}, u32[]{:S(2)}) %collective-permute-start.6) | collective-permute-done | bytes 81952 | tf_op jit(solution)/shard_map/ppermute | solution.py:14
  53.3 1.9 collective-permute-start.7
  55.2 3.1 %collective-permute-done.7 = bf16[4,64,128]{2,1,0:T(8,128)(2,1)S(1)} collective-permute-done((bf16[4,64,128]{2,1,0:T(8,128)(2,1)S(1)}, bf16[4,64,128]{2,1,0:T(8,128)(2,1)S(1)}, u32[]{:S(2)}, u32[]{:S(2)}) %collective-permute-start.7) | collective-permute-done | bytes 65568 | tf_op jit(solution)/shard_map/ppermute | solution.py:14
  58.3 1.9 collective-permute-start.8
  60.3 4.0 %collective-permute-done.8 = bf16[3,64,128]{2,1,0:T(8,128)(2,1)S(1)} collective-permute-done((bf16[3,64,128]{2,1,0:T(8,128)(2,1)S(1)}, bf16[3,64,128]{2,1,0:T(8,128)(2,1)S(1)}, u32[]{:S(2)}, u32[]{:S(2)}) %collective-permute-start.8) | collective-permute-done | bytes 49184 | tf_op jit(solution)/shard_map/ppermute | solution.py:14
  64.3 5.0 %collective-permute-start.9 = (bf16[2,64,128]{2,1,0:T(8,128)(2,1)S(1)}, bf16[2,64,128]{2,1,0:T(8,128)(2,1)S(1)}, u32[]{:S(2)}, u32[]{:S(2)}) collective-permute-start(bf16[2,64,128]{2,1,0:T(8,128)(2,1)S(1)} %get-tuple-element.9), channel_id=1, source_target_pairs={{0,4},{4,0},{1,5},{5,1},{2,6},{6,2},{3,7},{7,3},{8,12},{12,8},{9,1... | collective-permute-start | bytes 98312 | tf_op jit(solution)/shard_map/ppermute | solution.py:14
  69.3 3.7 %collective-permute-done.9 = bf16[2,64,128]{2,1,0:T(8,128)(2,1)S(1)} collective-permute-done((bf16[2,64,128]{2,1,0:T(8,128)(2,1)S(1)}, bf16[2,64,128]{2,1,0:T(8,128)(2,1)S(1)}, u32[]{:S(2)}, u32[]{:S(2)}) %collective-permute-start.9) | collective-permute-done | bytes 32800 | tf_op jit(solution)/shard_map/ppermute | solution.py:14
  73.0 10.9 %collective-permute-start.10 = (bf16[1,64,128]{2,1,0:T(8,128)(2,1)S(1)}, bf16[1,64,128]{2,1,0:T(8,128)(2,1)S(1)}, u32[]{:S(2)}, u32[]{:S(2)}) collective-permute-start(bf16[1,64,128]{2,1,0:T(8,128)(2,1)S(1)} %fusion.44), channel_id=1, source_target_pairs={{0,8},{8,0},{1,9},{9,1},{2,10},{10,2},{3,11},{11,3},{4,12},{12,4},... | collective-permute-start | bytes 49160 | tf_op jit(solution)/shard_map/ppermute | solution.py:14
  84.0 2.2 collective-permute-done.10
  86.2 0.7 convolution_bitcast_fusion.1
  87.0 5.3 %multiply_reduce_fusion.1 = (f32[64]{0:T(128)S(1)}, f32[64,1024]{1,0:T(8,128)S(1)}) fusion(f32[64,1024]{1,0:T(8,128)S(1)} %copy-done.4, f32[64,1024]{1,0:T(8,128)S(1)} %convolution_bitcast_fusion.1, f32[64,1024]{1,0:T(8,128)S(1)} %fusion.36, f32[64,1024]{1,0:T(8,128)S(1)} %collective-permute-done.1, f32[1024,1024]{1,0:T(8,128)S(1)} %fusion.39, ...), kind=kOutput, calls=%fused_computation.35 | convolution fusion | flops 810811328 | bytes 5513476 | tf_op jit(solution)/shard_map/dot_general | solution.py:30
  92.3 110.9 %all-reduce = (f32[64]{0:T(128)S(1)}, f32[64]{0:T(128)S(1)}) all-reduce(f32[64]{0:T(128)S(1)} %multiply_reduce_fusion.4, f32[64]{0:T(128)S(1)} %get-tuple-element.27), channel_id=1, replica_groups=mesh['leaf'=32,'top'=16] {'leaf','top'}, use_global_device_ids=true, to_apply=%region_1.0 | all-reduce | flops 128 | bytes 1024 | tf_op jit(solution)/shard_map/psum | solution.py:76
  203.1 0.2 multiply_reduce_fusion
  203.3 98.8 %psum.23 = f32[64]{0:T(128)S(1)} all-reduce(f32[64]{0:T(128)S(1)} %get-tuple-element.7), channel_id=1, replica_groups=mesh['leaf'=32,'top'=16] {'leaf','top'}, use_global_device_ids=true, to_apply=%region_7.0 | all-reduce | flops 64 | bytes 512 | tf_op jit(solution)/shard_map/psum | solution.py:81
  302.1 0.9 multiply_add_fusion
  (36 shorter events, 0.3 us)
Async XLA Ops:
  0.6 9.1 %copy-start = (bf16[8,1024,128]{2,1,0:T(8,128)(2,1)S(1)}, bf16[8,1024,128]{2,1,0:T(8,128)(2,1)}, u32[]{:S(2)}) copy-start(bf16[8,1024,128]{2,1,0:T(8,128)(2,1)} %param.13) | copy-start | bytes 6291460
  0.6 23.4 %copy-start.4 = (f32[64,1024]{1,0:T(8,128)S(1)}, f32[64,1024]{1,0:T(8,128)}, u32[]{:S(2)}) copy-start(f32[64,1024]{1,0:T(8,128)} %param.17) | copy-start | bytes 786436
  0.7 23.2 %copy-start.1 = (bf16[64,1024]{1,0:T(8,128)(2,1)S(1)}, bf16[64,1024]{1,0:T(8,128)(2,1)}, u32[]{:S(2)}) copy-start(bf16[64,1024]{1,0:T(8,128)(2,1)} %param.9) | copy-start | bytes 393220
  0.7 23.2 %copy-start.6 = (f32[64]{0:T(128)S(1)}, f32[64]{0:T(128)}, u32[]{:S(2)}) copy-start(f32[64]{0:T(128)} %param.10) | copy-start | bytes 772
  0.7 20.9 %copy-start.2 = (f32[64,1024]{1,0:T(8,128)S(1)}, f32[64,1024]{1,0:T(8,128)}, u32[]{:S(2)}) copy-start(f32[64,1024]{1,0:T(8,128)} %param.16) | copy-start | bytes 786436
  0.7 86.3 %collective-permute-start.1 = (f32[64,1024]{1,0:T(8,128)}, f32[64,1024]{1,0:T(8,128)S(1)}, u32[]{:S(2)}, u32[]{:S(2)}) collective-permute-start(f32[64,1024]{1,0:T(8,128)} %param.17), channel_id=1, source_target_pairs={{0,16},{16,0},{32,48},{48,32},{64,80},{80,64},{96,112},{112,96},{1... | collective-permute-start | bytes 786440 | tf_op jit(solution)/shard_map/ppermute | solution.py:14
  11.2 10.5 %collective-permute-start.2 = (bf16[8,64,128]{2,1,0:T(8,128)(2,1)S(1)}, bf16[8,64,128]{2,1,0:T(8,128)(2,1)S(1)}, u32[]{:S(2)}, u32[]{:S(2)}) collective-permute-start(bf16[8,64,128]{2,1,0:T(8,128)(2,1)S(1)} %get-tuple-element.25), channel_id=1, source_target_pairs={{0,16},{16,0},{32,48},{48,32},{64,80},{80,64},{96,112},{112,96},{1... | collective-permute-start | bytes 393224 | tf_op jit(solution)/shard_map/ppermute | solution.py:14
  13.1 10.8 %collective-permute-start = (bf16[64,1024]{1,0:T(8,128)(2,1)}, bf16[64,1024]{1,0:T(8,128)(2,1)S(1)}, u32[]{:S(2)}, u32[]{:S(2)}) collective-permute-start(bf16[64,1024]{1,0:T(8,128)(2,1)} %param.9), channel_id=1, source_target_pairs={{0,16},{16,0},{32,48},{48,32},{64,80},{80,64},{96,112},{112,96},{1... | collective-permute-start | bytes 393224 | tf_op jit(solution)/shard_map/ppermute | solution.py:14
  21.8 11.1 %collective-permute-start.3 = (bf16[8,64,128]{2,1,0:T(8,128)(2,1)S(1)}, bf16[8,64,128]{2,1,0:T(8,128)(2,1)S(1)}, u32[]{:S(2)}, u32[]{:S(2)}) collective-permute-start(bf16[8,64,128]{2,1,0:T(8,128)(2,1)S(1)} %get-tuple-element.21), channel_id=1, source_target_pairs={{0,32},{32,0},{16,48},{48,16},{64,96},{96,64},{80,112},{112,80},{1... | collective-permute-start | bytes 393224 | tf_op jit(solution)/shard_map/ppermute | solution.py:14
  29.3 57.0 %copy-start.7 = (f32[8,128]{1,0:T(8,128)S(1)}, f32[8,128]{1,0:T(8,128)}, u32[]{:S(2)}) copy-start(f32[8,128]{1,0:T(8,128)} %param.14) | copy-start | bytes 12292
  33.0 8.2 %collective-permute-start.4 = (bf16[7,64,128]{2,1,0:T(8,128)(2,1)S(1)}, bf16[7,64,128]{2,1,0:T(8,128)(2,1)S(1)}, u32[]{:S(2)}, u32[]{:S(2)}) collective-permute-start(bf16[7,64,128]{2,1,0:T(8,128)(2,1)S(1)} %get-tuple-element.19), channel_id=1, source_target_pairs={{0,64},{64,0},{16,80},{80,16},{32,96},{96,32},{48,112},{112,48},{1... | collective-permute-start | bytes 344072 | tf_op jit(solution)/shard_map/ppermute | solution.py:14
  41.2 5.4 %collective-permute-start.5 = (bf16[6,64,128]{2,1,0:T(8,128)(2,1)S(1)}, bf16[6,64,128]{2,1,0:T(8,128)(2,1)S(1)}, u32[]{:S(2)}, u32[]{:S(2)}) collective-permute-start(bf16[6,64,128]{2,1,0:T(8,128)(2,1)S(1)} %get-tuple-element.17), channel_id=1, source_target_pairs={{0,128},{128,0},{16,144},{144,16},{32,160},{160,32},{48,176},{176,... | collective-permute-start | bytes 294920 | tf_op jit(solution)/shard_map/ppermute | solution.py:14
  46.6 6.7 %collective-permute-start.6 = (bf16[5,64,128]{2,1,0:T(8,128)(2,1)S(1)}, bf16[5,64,128]{2,1,0:T(8,128)(2,1)S(1)}, u32[]{:S(2)}, u32[]{:S(2)}) collective-permute-start(bf16[5,64,128]{2,1,0:T(8,128)(2,1)S(1)} %get-tuple-element.15), channel_id=1, source_target_pairs={{0,256},{256,0},{16,272},{272,16},{32,288},{288,32},{48,304},{304,... | collective-permute-start | bytes 245768 | tf_op jit(solution)/shard_map/ppermute | solution.py:14
  53.3 5.0 %collective-permute-start.7 = (bf16[4,64,128]{2,1,0:T(8,128)(2,1)S(1)}, bf16[4,64,128]{2,1,0:T(8,128)(2,1)S(1)}, u32[]{:S(2)}, u32[]{:S(2)}) collective-permute-start(bf16[4,64,128]{2,1,0:T(8,128)(2,1)S(1)} %get-tuple-element.13), channel_id=1, source_target_pairs={{0,1},{1,0},{2,3},{3,2},{4,5},{5,4},{6,7},{7,6},{8,9},{9,8},{10,11... | collective-permute-start | bytes 196616 | tf_op jit(solution)/shard_map/ppermute | solution.py:14
  58.3 6.0 %collective-permute-start.8 = (bf16[3,64,128]{2,1,0:T(8,128)(2,1)S(1)}, bf16[3,64,128]{2,1,0:T(8,128)(2,1)S(1)}, u32[]{:S(2)}, u32[]{:S(2)}) collective-permute-start(bf16[3,64,128]{2,1,0:T(8,128)(2,1)S(1)} %get-tuple-element.11), channel_id=1, source_target_pairs={{0,2},{2,0},{1,3},{3,1},{4,6},{6,4},{5,7},{7,5},{8,10},{10,8},{9,1... | collective-permute-start | bytes 147464 | tf_op jit(solution)/shard_map/ppermute | solution.py:14
  64.3 8.7 %collective-permute-start.9 = (bf16[2,64,128]{2,1,0:T(8,128)(2,1)S(1)}, bf16[2,64,128]{2,1,0:T(8,128)(2,1)S(1)}, u32[]{:S(2)}, u32[]{:S(2)}) collective-permute-start(bf16[2,64,128]{2,1,0:T(8,128)(2,1)S(1)} %get-tuple-element.9), channel_id=1, source_target_pairs={{0,4},{4,0},{1,5},{5,1},{2,6},{6,2},{3,7},{7,3},{8,12},{12,8},{9,1... | collective-permute-start | bytes 98312 | tf_op jit(solution)/shard_map/ppermute | solution.py:14
  73.0 13.2 %collective-permute-start.10 = (bf16[1,64,128]{2,1,0:T(8,128)(2,1)S(1)}, bf16[1,64,128]{2,1,0:T(8,128)(2,1)S(1)}, u32[]{:S(2)}, u32[]{:S(2)}) collective-permute-start(bf16[1,64,128]{2,1,0:T(8,128)(2,1)S(1)} %fusion.44), channel_id=1, source_target_pairs={{0,8},{8,0},{1,9},{9,1},{2,10},{10,2},{3,11},{11,3},{4,12},{12,4},... | collective-permute-start | bytes 49160 | tf_op jit(solution)/shard_map/ppermute | solution.py:14
  87.0 215.2 %copy-start.5 = (f32[64,1024]{1,0:T(8,128)S(1)}, f32[64,1024]{1,0:T(8,128)}, u32[]{:S(2)}) copy-start(f32[64,1024]{1,0:T(8,128)} %param.15) | copy-start | bytes 786436
  203.3 99.7 %copy-start.3 = (f32[64,1024]{1,0:T(8,128)}, f32[64,1024]{1,0:T(8,128)S(1)}, u32[]{:S(2)}) copy-start(f32[64,1024]{1,0:T(8,128)S(1)} %get-tuple-element.8) | copy-start | bytes 786436
where the time goes:
time: 304 us; the launch traced here: 303 us
  blocking collectives  210 us (69%)
  starting transfers between devices  41 us (13%)
  waiting for transfers between devices  27.4 us (9%)
  matrix products  21 us (7%)
    psum x1, blocking collectives, local(): norm_now = lax.psum(jnp.sum(residual * residual, axis=1), ('leaf', 'top'))  111 us
    psum x1, blocking collectives, local(): lax.psum(jnp.sum(new_residual * new_residual, axis=1), ('leaf', 'top'))  98.8 us
    ppermute x11, starting transfers between devices, partner(): return lax.ppermute(block, axis, route)  41 us
    ppermute x11, waiting for transfers between devices, partner(): return lax.ppermute(block, axis, route)  27.4 us
    dot_general x2, matrix products, leaf_part(): lax.dot_general(other_dir, kernel, (((1,), (1,)), ((), ())), precision=la...  10.5 us
    dot_general x2, matrix products, leaf_part(): lax.dot_general(own_scaled, other_scaled, (((0,), (0,)), ((), ())), preci...  8.39 us
  transfers between devices with their start and end apart: 11, of which 7 were waited for; matrix products, arithmetic and copies ran while one was open for 5% of the time, Pallas kernels for 0%

commit v1 on v0

v1 whole, which is shorter than its diff:
```python
import jax
import jax.numpy as jnp
import numpy as np
from jax import lax
from jax.experimental import pallas as pl
from jax.experimental.pallas import tpu as pltpu
from jax.sharding import Mesh, PartitionSpec as P

LOG2E = 1.4426950408889634
CHIP = ("x", "y")
LEAF = ("x", "y", "core")
BF = jnp.bfloat16
F32 = jnp.float32


def parts_of(value, count):
    parts = []
    for _ in range(count):
        part = value.astype(BF)
        parts.append(part)
        value = value - part.astype(F32)
    return parts


def leaf_kernel(signal_ref, rate_ref, own_ref, other_ref, out_ref):
    points = own_ref.shape[1]
    rate = rate_ref[...]
    row = lax.broadcasted_iota(jnp.int32, (16, points), 0)
    ones = jnp.where(row < 3, 1.0, 0.0).astype(BF)

    def prepared(ref):
        feat = ref[0:64, :]
        wide = feat.astype(F32)
        scaled = wide * rate
        half = -0.5 * jnp.sum(wide * scaled, axis=0, keepdims=True)
        one, two, three = [part.astype(F32) for part in parts_of(half, 3)]
        halves = jnp.where(row == 0, one, jnp.where(row == 1, two, jnp.where(row == 2, three, 0.0)))
        return feat, scaled, halves.astype(BF)

    feat, scaled, halves = prepared(own_ref)
    other_feat, _, other_halves = prepared(other_ref)
    left = jnp.concatenate(parts_of(scaled, 3) + [halves, ones], axis=0).T
    right = [
        jnp.concatenate([feat, feat, feat, ones, halves], axis=0),
        jnp.concatenate([other_feat, other_feat, other_feat, ones, other_halves], axis=0),
    ]
    values = [own_ref[64:192, :], other_ref[64:192, :]]
    tile = 256
    for start in range(0, points, tile):
        both = jnp.zeros((tile, 128), F32)
        low = jnp.zeros((tile, 64), F32)
        for side in range(2):
            power = jnp.dot(left[start : start + tile], right[side], preferred_element_type=F32)
            kernel = jnp.exp2(power)
            high_part, low_part = parts_of(kernel, 2)
            dims = (((1,), (1,)), ((), ()))
            both += lax.dot_general(high_part, values[side], dims, preferred_element_type=F32)
            low += lax.dot_general(low_part, values[side][0:64], dims, preferred_element_type=F32)
        turned = both.T
        out_ref[:, start : start + tile] = signal_ref[0] * (turned[0:64] + turned[64:128] + low.T)


def leaf_term(signal, rate, own, other):
    return pl.pallas_call(
        leaf_kernel,
        out_shape=jax.ShapeDtypeStruct((64, own.shape[1]), F32),
        in_specs=[pl.BlockSpec(memory_space=pltpu.SMEM)] + [pl.BlockSpec(memory_space=pltpu.VMEM)] * 3,
        out_specs=pl.BlockSpec(memory_space=pltpu.VMEM),
        compiler_params=pltpu.CompilerParams(vmem_limit_bytes=40 * 1024 * 1024),
        cost_estimate=pl.CostEstimate(
            flops=2 * 1024 * 2048 * 256 * 3, bytes_accessed=2**20, transcendentals=1024 * 2048
        ),
    )(signal, rate, own, other)


def level_mask(count, mine):
    other = jnp.arange(count, dtype=jnp.int32)[:, None]
    low = jnp.left_shift(1, jnp.arange(4, dtype=jnp.int32))[None, :]
    apart = jnp.bitwise_xor(other, mine)
    return ((apart >= low) & (apart < 2 * low)).astype(BF)


def local(
    features, lengthscale, signal_var, noise_var, factors, gains, solution, residual, direction
):
    core = lax.axis_index("core")
    chip = lax.axis_index(CHIP)
    plane = lax.axis_index("z")

    direction_low, direction_rest = parts_of(direction, 2)
    own = jnp.concatenate([features, direction_low, direction_rest], axis=0)
    other = lax.ppermute(own, "core", [(0, 1), (1, 0)])

    projection = jnp.einsum(
        "cp,lpr->lcr", direction_low, factors, preferred_element_type=F32
    ).astype(BF)
    near = level_mask(16, chip)
    far = level_mask(16, plane)
    near_out = jnp.einsum("jk,khcr->jhcr", near, projection[:4].reshape(4, 2, 32, 128))
    far_out = projection[4:].reshape(4, 2, 32, 128).transpose(2, 0, 1, 3)
    sent = jnp.concatenate([near_out.reshape(32, 32, 128), far_out.reshape(32, 8, 128)], axis=1)
    got = lax.all_to_all(sent, LEAF, 0, 0, tiled=True)

    rate = (LOG2E / (lengthscale * lengthscale))[:, None]
    image = noise_var[0] * direction + leaf_term(signal_var, rate, own, other)

    plane_sum = jnp.sum(got[:, 32:].astype(F32), axis=0).astype(BF).reshape(4, 2, 128)
    far_sent = jnp.einsum("jk,kcr->jcr", far, plane_sum)
    far_got = lax.all_to_all(far_sent, "z", 0, 0, tiled=True)

    near_sum = jnp.einsum(
        "jk,jhcr->kcr", near, got[:, :32].reshape(16, 2, 32, 128), preferred_element_type=F32
    )
    near_weighted = (gains[:4, None, :] * near_sum).astype(BF)
    near_other = lax.ppermute(near_weighted, "core", [(0, 1), (1, 0)])
    near_all = jnp.where(
        core == 0,
        jnp.concatenate([near_weighted, near_other], axis=1),
        jnp.concatenate([near_other, near_weighted], axis=1),
    )

    far_sum = jnp.einsum("jk,jcr->kcr", far, far_got, preferred_element_type=F32)
    far_weighted = (gains[4:, None, :] * far_sum).astype(BF)
    far_all = lax.all_to_all(
        jnp.broadcast_to(far_weighted[None], (32, 4, 2, 128)), LEAF, 0, 0, tiled=True
    )
    far_all = far_all.transpose(1, 2, 0, 3).reshape(4, 64, 128)
    weighted = jnp.concatenate([near_all, far_all], axis=0)

    image = image + jnp.einsum("lcr,lpr->cp", weighted, factors, preferred_element_type=F32)

    def total(stats):
        stats = lax.all_to_all(
            jnp.broadcast_to(stats[None], (16,) + stats.shape), CHIP, 0, 0, tiled=True
        ).sum(0)
        return lax.all_to_all(
            jnp.broadcast_to(stats[None], (32,) + stats.shape), ("core", "z"), 0, 0, tiled=True
        ).sum(0)

    stats = jnp.stack(
        [
            jnp.sum(residual * residual, axis=1),
            jnp.sum(direction * image, axis=1),
            jnp.sum(residual * image, axis=1),
            jnp.sum(image * image, axis=1),
        ]
    )
    norm_now, curvature, cross, square = total(stats.reshape(1, 256)).reshape(4, 64)
    step_size = norm_now / curvature
    norm_next = jnp.maximum(norm_now + step_size * (step_size * square - 2.0 * cross), 0.0)
    new_solution = solution + step_size[:, None] * direction
    new_residual = residual - step_size[:, None] * image
    new_direction = new_residual + (norm_next / norm_now)[:, None] * direction
    return (new_solution, new_residual, new_direction)


def solution(mesh):
    fine = Mesh(mesh.devices.reshape(4, 4, 2, 16), ("x", "y", "core", "z"))
    points = P(None, ("z", "x", "y", "core"))
    return jax.shard_map(
        local,
        mesh=fine,
        in_specs=(
            points,
            P(),
            P(),
            P(),
            P(None, ("z", "x", "y", "core"), None),
            P(),
            points,
            points,
            points,
        ),
        out_specs=(points, points, points),
        check_vma=False,
    )
```

time: 304 us -> 95.4 us (0.31)
  blocking collectives: 210 us -> 27 us
  matrix products: 21 us -> 3.38 us
  waiting for transfers between devices: 27.4 us -> 17.8 us
  starting transfers between devices: 41 us -> 32.8 us
  other arithmetic: 1.61 us -> 5.8 us
  Pallas kernels: 0 us -> 3.67 us
    psum x2 -> x0, blocking collectives: 210 us -> none  [the longest x1 111 us: local(): norm_now = lax.psum(jnp.sum(residual * residual, axis=1), ('leaf', 'top'))]
    ppermute x11 -> x2, starting transfers between devices: 41 us -> 4.45 us  [the longest x1 2.26 us: local(): other = lax.ppermute(own, 'core', [(0, 1), (1, 0)])]
    all_to_all x0 -> x3, starting transfers between devices: none -> 28.4 us  [the longest x1 13 us: local(): far_got = lax.all_to_all(far_sent, 'z', 0, 0, tiled=True)]
    ppermute x11 -> x2, waiting for transfers between devices: 27.4 us -> 0.01 us  [the longest x1 0.01 us: local(): other = lax.ppermute(own, 'core', [(0, 1), (1, 0)])]
    all_to_all x0 -> x2, blocking collectives: none -> 27 us  [the longest x1 17 us: total(): lax.all_to_all(jnp.broadcast_to(stats[None], (32,) + stats.shape), ('core...]
    all_to_all x0 -> x3, waiting for transfers between devices: none -> 17.8 us  [the longest x1 8.77 us: local(): far_got = lax.all_to_all(far_sent, 'z', 0, 0, tiled=True)]
    dot_general x5, matrix products: 19.6 us -> 2.91 us  [the longest x1 1.87 us: local(): jnp.einsum('lcr,lpr->cp', weighted, factors, preferred_element_type=F32)]
    pallas_call x0 -> x1, Pallas kernels: none -> 3.67 us  [leaf_term(): pl.pallas_call(leaf_kernel, out_shape=jax.ShapeDtypeStruct((64, own.shape...]
  transfers between devices with their start and end apart: 11 -> 5, of which waited for: 7 -> 3; matrix products, arithmetic and copies ran while one was open for 5% -> 3% of each run, Pallas kernels for 0% -> 4%
where the time goes in v1:
time: 95.4 us; the launch traced here: 94.8 us
  starting transfers between devices  32.8 us (34%)
  blocking collectives  27 us (28%)
  waiting for transfers between devices  17.8 us (19%)
  other arithmetic  5.8 us (6%)
  Pallas kernels  3.67 us (4%)
  matrix products  3.38 us (4%)
  between operations  2.2 us (2%)
  local copies, waits for them, and re-layouts  2.16 us (2%)
    all_to_all x1, blocking collectives, total(): lax.all_to_all(jnp.broadcast_to(stats[None], (32,) + stats.shape), ('core...  17 us
    all_to_all x1, starting transfers between devices, local(): far_got = lax.all_to_all(far_sent, 'z', 0, 0, tiled=True)  13 us
    all_to_all x1, starting transfers between devices, local(): got = lax.all_to_all(sent, LEAF, 0, 0, tiled=True)  10.4 us
    all_to_all x1, blocking collectives, total(): lax.all_to_all(jnp.broadcast_to(stats[None], (16,) + stats.shape), CHIP,...  10 us
    all_to_all x1, waiting for transfers between devices, local(): far_got = lax.all_to_all(far_sent, 'z', 0, 0, tiled=True)  8.77 us
    all_to_all x1, waiting for transfers between devices, local(): got = lax.all_to_all(sent, LEAF, 0, 0, tiled=True)  5.98 us
    all_to_all x1, starting transfers between devices, local(): lax.all_to_all(jnp.broadcast_to(far_weighted[None], (32, 4, 2, 128)), LEA...  5 us
    pallas_call x1, Pallas kernels, leaf_term(): pl.pallas_call(leaf_kernel, out_shape=jax.ShapeDtypeStruct((64, own.shape...  3.67 us
  transfers between devices with their start and end apart: 5, of which 3 were waited for; matrix products, arithmetic and copies ran while one was open for 3% of the time, Pallas kernels for 4%

profile of v1, /device:TPU:1, one launch (start us, length us, event | category | flops | bytes accessed | tf_op | source)
XLA Modules:
  0.0 94.8 jit_solution(10896143209101684821)
XLA Ops:
  0.6 0.0 copy-start
  0.7 1.2 %subtract_convert_fusion = (bf16[64,1024]{1,0:T(8,128)(2,1)S(1)}, bf16[64,1024]{1,0:T(8,128)(2,1)S(1)}) fusion(f32[64,1024]{1,0:T(8,128)} %param.17), kind=kLoop, calls=%fused_computation.18 | loop fusion | flops 262144 | bytes 524288 | tf_op jit(solution)/shard_map/convert_element_type | solution.py:19
  1.9 0.5 copy-done
  2.4 0.5 fusion
  2.9 0.4 fusion.8
  3.3 0.1 copy.52
  3.4 0.1 copy.53
  3.4 0.7 pad_maximum_fusion.1
  4.2 10.4 %all-to-all-start = ((bf16[32,40,128]{2,1,0:T(8,128)(2,1)}), bf16[32,40,128]{2,1,0:T(8,128)(2,1)S(1)}, u32[]{:S(2)}, u32[]{:S(2)}) async-start(bf16[32,40,128]{2,1,0:T(8,128)(2,1)} %pad_maximum_fusion.1), calls=%async_computation | async-start | bytes 655360 | tf_op jit(solution)/shard_map/all_to_all | solution.py:102
  14.6 2.3 %collective-permute-start = (bf16[192,1024]{1,0:T(8,128)(2,1)S(1)}, bf16[192,1024]{1,0:T(8,128)(2,1)S(1)}, u32[]{:S(2)}, u32[]{:S(2)}) collective-permute-start(bf16[192,1024]{1,0:T(8,128)(2,1)S(1)} %pad_maximum_fusion.own_ref), channel_id=1, source_target_pairs={{0,16},{16,0},{1,17},{17,1},{2,18},{18,2},{3,19},{19,3},{4,20},{20... | collective-permute-start | bytes 1179656 | tf_op jit(solution)/shard_map/ppermute | solution.py:92
  16.9 0.1 copy.50.rate_ref
  18.4 6.0 %all-to-all-done = bf16[32,40,128]{2,1,0:T(8,128)(2,1)S(1)} async-done(((bf16[32,40,128]{2,1,0:T(8,128)(2,1)}), bf16[32,40,128]{2,1,0:T(8,128)(2,1)S(1)}, u32[]{:S(2)}, u32[]{:S(2)}) %all-to-all-start) | async-done | bytes 327712 | tf_op jit(solution)/shard_map/all_to_all | solution.py:102
  24.4 0.3 fusion.11
  24.6 0.6 copy.56
  25.2 13.0 %all-to-all-start.1 = ((bf16[16,2,128]{2,1,0:T(2,128)(2,1)}), bf16[16,2,128]{2,1,0:T(2,128)(2,1)S(1)}, u32[]{:S(2)}, u32[]{:S(2)}) async-start(bf16[16,2,128]{2,1,0:T(2,128)(2,1)} %copy.56), calls=%async_computation.1 | async-start | bytes 16384 | tf_op jit(solution)/shard_map/all_to_all | solution.py:109
  38.3 0.2 fusion.1
  38.5 2.2 %collective-permute-start.1 = (bf16[4,32,128]{2,0,1:T(4,128)(2,1)S(1)}, bf16[4,32,128]{2,0,1:T(4,128)(2,1)S(1)}, u32[]{:S(2)}, u32[]{:S(2)}) collective-permute-start(bf16[4,32,128]{2,0,1:T(4,128)(2,1)S(1)} %fusion.1), channel_id=1, source_target_pairs={{0,16},{16,0},{1,17},{17,1},{2,18},{18,2},{3,19},{19,3},{4,20},{20... | collective-permute-start | bytes 98312 | tf_op jit(solution)/shard_map/ppermute | solution.py:115
  40.7 8.8 %all-to-all-done.1 = bf16[16,2,128]{2,1,0:T(2,128)(2,1)S(1)} async-done(((bf16[16,2,128]{2,1,0:T(2,128)(2,1)}), bf16[16,2,128]{2,1,0:T(2,128)(2,1)S(1)}, u32[]{:S(2)}, u32[]{:S(2)}) %all-to-all-start.1) | async-done | bytes 8224 | tf_op jit(solution)/shard_map/all_to_all | solution.py:109
  49.5 0.2 fusion.2
  49.7 0.7 broadcast_in_dim.11
  50.3 5.0 %all-to-all-start.2 = ((bf16[32,4,2,128]{3,1,2,0:T(4,128)(2,1)}), bf16[32,4,2,128]{3,1,2,0:T(4,128)(2,1)S(1)}, u32[]{:S(2)}, u32[]{:S(2)}) async-start(bf16[32,4,2,128]{3,1,2,0:T(4,128)(2,1)} %broadcast_in_dim.11), calls=%async_computation.2 | async-start | bytes 131072 | tf_op jit(solution)/shard_map/all_to_all | solution.py:124
  55.3 0.7 maximum_select_fusion
  56.0 3.7 %shard_map.112 = f32[64,1024]{1,0:T(8,128)S(1)} custom-call(f32[1]{0:T(128)S(6)} %copy.79.signal_ref, f32[64,1]{1,0:T(8,128)S(1)} %copy.50.rate_ref, bf16[192,1024]{1,0:T(8,128)(2,1)S(1)} %pad_maximum_fusion.own_ref, bf16[192,1024]{1,0:T(8,128)(2,1)S(1)} %collective-permute-done.other_ref), custom_call_target="tpu_custom_call" | custom-call | flops 3221225472 | bytes 1048576 | tf_op jit(solution)/shard_map/pallas_call | solution.py:64
  59.7 3.0 %all-to-all-done.2 = bf16[32,4,2,128]{3,1,2,0:T(4,128)(2,1)S(1)} async-done(((bf16[32,4,2,128]{3,1,2,0:T(4,128)(2,1)}), bf16[32,4,2,128]{3,1,2,0:T(4,128)(2,1)S(1)}, u32[]{:S(2)}, u32[]{:S(2)}) %all-to-all-start.2) | async-done | bytes 65568 | tf_op jit(solution)/shard_map/all_to_all | solution.py:124
  62.7 0.9 pad_maximum_fusion.2
  63.7 1.9 %multiply_reduce_fusion.3 = (f32[64]{0:T(128)S(1)}, f32[64]{0:T(128)S(1)}, f32[64]{0:T(128)S(1)}, f32[64]{0:T(128)S(1)}, f32[64,1024]{1,0:T(8,128)S(1)}) fusion(f32[64,1024]{1,0:T(8,128)} %param.16, f32[64,1024]{1,0:T(8,128)S(1)} %copy-done.1, bf16[8,1024,128]{2,1,0:T(8,128)(2,1)S(1)} %copy-done, bf16[8,64,128]{2,0,1:T(8,128)(2,1)S(1)} %pad_maximum_fusion.2, ...), kind=kOutput, calls=%fused_computation.19 | convolution fusion | flops 134938368 | bytes 3277828 | tf_op jit(solution)/shard_map/lcr,lpr->cp/dot_general | solution.py:130
  65.6 0.1 broadcast_in_dim.12
  65.7 10.0 %all_to_all.25 = f32[16,1,256]{2,1,0:T(1,128)S(1)} all-to-all(f32[16,1,256]{2,1,0:T(1,128)S(1)} %broadcast_in_dim.13), channel_id=1, replica_groups=mesh['x'=4,'y'=4,'core'=2,'z'=16] {'x','y'}, dimensions={0} | all-to-all | bytes 32768 | tf_op jit(solution)/shard_map/all_to_all | solution.py:133
  75.7 17.0 %all_to_all.26 = f32[32,1,256]{2,1,0:T(1,128)S(1)} all-to-all(f32[32,1,256]{2,1,0:T(1,128)S(1)} %broadcast_in_dim.14), channel_id=1, replica_groups=mesh['x'=4,'y'=4,'core'=2,'z'=16] {'core','z'}, dimensions={0} | all-to-all | bytes 65536 | tf_op jit(solution)/shard_map/all_to_all | solution.py:136
  92.7 0.1 reduce_sum.84
  92.8 0.1 maximum_divide_fusion
  92.8 2.0 %multiply_add_fusion = (f32[64,1024]{1,0:T(8,128)}, f32[64,1024]{1,0:T(8,128)}, f32[64,1024]{1,0:T(8,128)}) fusion(f32[64,1024]{1,0:T(8,128)S(1)} %copy-done.1, f32[64]{0:T(128)S(1)} %get-tuple-element.9, f32[64,1024]{1,0:T(8,128)S(1)} %copy-done.2, f32[64,1024]{1,0:T(8,128)S(1)} %get-tuple-element.18, f32[64]{0:T(128)S(1)} %get-tuple-element.10, ...), kind=kLoop, calls=%fused_computation.11 | loop fusion | flops 393216 | bytes 1835520 | tf_op jit(solution)/shard_map/add | solution.py:153
  (26 shorter events, 0.3 us)
Async XLA Ops:
  0.6 1.8 %copy-start = (bf16[8,1024,128]{2,1,0:T(8,128)(2,1)S(1)}, bf16[8,1024,128]{2,1,0:T(8,128)(2,1)}, u32[]{:S(2)}) copy-start(bf16[8,1024,128]{2,1,0:T(8,128)(2,1)} %param.13) | copy-start | bytes 6291460
  2.4 12.2 %copy-start.3 = (bf16[64,1024]{1,0:T(8,128)(2,1)S(1)}, bf16[64,1024]{1,0:T(8,128)(2,1)}, u32[]{:S(2)}) copy-start(bf16[64,1024]{1,0:T(8,128)(2,1)} %param.9) | copy-start | bytes 393220
  2.9 14.0 %copy-start.5 = (f32[64]{0:T(128)S(1)}, f32[64]{0:T(128)}, u32[]{:S(2)}) copy-start(f32[64]{0:T(128)} %param.10) | copy-start | bytes 772
  2.9 15.4 %copy-start.4 = (f32[8,128]{1,0:T(8,128)S(1)}, f32[8,128]{1,0:T(8,128)}, u32[]{:S(2)}) copy-start(f32[8,128]{1,0:T(8,128)} %param.14) | copy-start | bytes 12292
  4.2 20.2 %all-to-all-start = ((bf16[32,40,128]{2,1,0:T(8,128)(2,1)}), bf16[32,40,128]{2,1,0:T(8,128)(2,1)S(1)}, u32[]{:S(2)}, u32[]{:S(2)}) async-start(bf16[32,40,128]{2,1,0:T(8,128)(2,1)} %pad_maximum_fusion.1), calls=%async_computation | async-start | bytes 655360 | tf_op jit(solution)/shard_map/all_to_all | solution.py:102
  14.6 41.4 %collective-permute-start = (bf16[192,1024]{1,0:T(8,128)(2,1)S(1)}, bf16[192,1024]{1,0:T(8,128)(2,1)S(1)}, u32[]{:S(2)}, u32[]{:S(2)}) collective-permute-start(bf16[192,1024]{1,0:T(8,128)(2,1)S(1)} %pad_maximum_fusion.own_ref), channel_id=1, source_target_pairs={{0,16},{16,0},{1,17},{17,1},{2,18},{18,2},{3,19},{19,3},{4,20},{20... | collective-permute-start | bytes 1179656 | tf_op jit(solution)/shard_map/ppermute | solution.py:92
  25.2 24.2 %all-to-all-start.1 = ((bf16[16,2,128]{2,1,0:T(2,128)(2,1)}), bf16[16,2,128]{2,1,0:T(2,128)(2,1)S(1)}, u32[]{:S(2)}, u32[]{:S(2)}) async-start(bf16[16,2,128]{2,1,0:T(2,128)(2,1)} %copy.56), calls=%async_computation.1 | async-start | bytes 16384 | tf_op jit(solution)/shard_map/all_to_all | solution.py:109
  38.5 16.8 %collective-permute-start.1 = (bf16[4,32,128]{2,0,1:T(4,128)(2,1)S(1)}, bf16[4,32,128]{2,0,1:T(4,128)(2,1)S(1)}, u32[]{:S(2)}, u32[]{:S(2)}) collective-permute-start(bf16[4,32,128]{2,0,1:T(4,128)(2,1)S(1)} %fusion.1), channel_id=1, source_target_pairs={{0,16},{16,0},{1,17},{17,1},{2,18},{18,2},{3,19},{19,3},{4,20},{20... | collective-permute-start | bytes 98312 | tf_op jit(solution)/shard_map/ppermute | solution.py:115
  50.3 12.4 %all-to-all-start.2 = ((bf16[32,4,2,128]{3,1,2,0:T(4,128)(2,1)}), bf16[32,4,2,128]{3,1,2,0:T(4,128)(2,1)S(1)}, u32[]{:S(2)}, u32[]{:S(2)}) async-start(bf16[32,4,2,128]{3,1,2,0:T(4,128)(2,1)} %broadcast_in_dim.11), calls=%async_computation.2 | async-start | bytes 131072 | tf_op jit(solution)/shard_map/all_to_all | solution.py:124
  56.0 7.7 %copy-start.1 = (f32[64,1024]{1,0:T(8,128)S(1)}, f32[64,1024]{1,0:T(8,128)}, u32[]{:S(2)}) copy-start(f32[64,1024]{1,0:T(8,128)} %param.17) | copy-start | bytes 786436
  59.7 33.1 %copy-start.2 = (f32[64,1024]{1,0:T(8,128)S(1)}, f32[64,1024]{1,0:T(8,128)}, u32[]{:S(2)}) copy-start(f32[64,1024]{1,0:T(8,128)} %param.16) | copy-start | bytes 786436

commit v2 on v1

v2 whole, which is shorter than its diff:
```python
import jax
import jax.numpy as jnp
import numpy as np
from jax import lax
from jax.experimental import pallas as pl
from jax.experimental.pallas import tpu as pltpu
from jax.sharding import Mesh, PartitionSpec as P

LOG2E = 1.4426950408889634
CHIP = ("x", "y")
LEAF = ("x", "y", "core")
ROW = ("y", "core")
VMEM = pl.BlockSpec(memory_space=pltpu.VMEM)
SMEM = pl.BlockSpec(memory_space=pltpu.SMEM)
HBM = pl.BlockSpec(memory_space=pltpu.HBM)
SWAP = [(0, 1), (1, 0)]
BF = jnp.bfloat16
F32 = jnp.float32


def parts_of(value, count):
    parts = []
    for _ in range(count):
        part = value.astype(BF)
        parts.append(part)
        value = value - part.astype(F32)
    return parts


def leaf_kernel(signal_ref, rate_ref, own_ref, other_ref, *refs):
    out_ref = refs[-1]
    points = own_ref.shape[1]
    rate = rate_ref[...]
    row = lax.broadcasted_iota(jnp.int32, (16, points), 0)
    ones = jnp.where(row < 3, 1.0, 0.0).astype(BF)

    def prepared(ref):
        feat = ref[0:64, :]
        wide = feat.astype(F32)
        scaled = wide * rate
        half = -0.5 * jnp.sum(wide * scaled, axis=0, keepdims=True)
        one, two, three = [part.astype(F32) for part in parts_of(half, 3)]
        halves = jnp.where(row == 0, one, jnp.where(row == 1, two, jnp.where(row == 2, three, 0.0)))
        return feat, scaled, halves.astype(BF)

    _, scaled, halves = prepared(own_ref)
    feat, _, other_halves = prepared(other_ref)
    left = jnp.concatenate(parts_of(scaled, 3) + [halves, ones], axis=0).T
    right = jnp.concatenate([feat, feat, feat, ones, other_halves], axis=0)
    value = other_ref[64:192, :]
    dims = (((1,), (1,)), ((), ()))
    tile = 256
    for start in range(0, points, tile):
        here = slice(start, start + tile)
        power = jnp.dot(left[here], right, preferred_element_type=F32)
        high, low = parts_of(jnp.exp2(power), 2)
        both = lax.dot_general(high, value, dims, preferred_element_type=F32).T
        rest = lax.dot_general(low, value[0:64], dims, preferred_element_type=F32).T
        result = signal_ref[0] * (both[0:64] + both[64:128] + rest)
        if len(refs) > 1:
            result += refs[0][:, here]
        out_ref[:, here] = result


def leaf_term(signal, rate, own, other, *base):
    return pl.pallas_call(
        leaf_kernel,
        out_shape=jax.ShapeDtypeStruct((64, own.shape[1]), F32),
        in_specs=[SMEM] + [VMEM] * (3 + len(base)),
        out_specs=VMEM,
        compiler_params=pltpu.CompilerParams(vmem_limit_bytes=40 * 2**20),
        cost_estimate=pl.CostEstimate(
            flops=2 * 1024 * 1024 * 256 * 3, bytes_accessed=2**20, transcendentals=1024 * 1024
        ),
    )(signal, rate, own, other, *base)


def image_kernel(
    place_ref,
    noise_ref,
    near_ref,
    near_other_ref,
    far_ref,
    factors_ref,
    leaf_ref,
    direction_ref,
    residual_ref,
    image_ref,
    stats_ref,
):
    first = place_ref[0] == 0
    levels = []
    for k in range(4):
        own, other = near_ref[k].astype(F32), near_other_ref[k].astype(F32)
        low = jnp.where(first, own, other)
        high = jnp.where(first, other, own)
        levels.append(jnp.concatenate([low, high], axis=0).astype(BF))
    levels += [far_ref[k] for k in range(4)]
    pairs = [jnp.concatenate(levels[k : k + 2], axis=1) for k in range(0, 8, 2)]
    points = direction_ref.shape[1]
    tile = 256
    sums = [jnp.zeros((64, 128), F32) for _ in range(4)]
    for start in range(0, points, tile):
        here = slice(start, start + tile)
        direction, residual = direction_ref[:, here], residual_ref[:, here]
        image = noise_ref[0] * direction + leaf_ref[:, here]
        for k in range(0, 8, 2):
            basis = jnp.concatenate([factors_ref[k, here, :], factors_ref[k + 1, here, :]], axis=1)
            image += lax.dot_general(
                pairs[k // 2], basis, (((1,), (1,)), ((), ())), preferred_element_type=F32
            )
        image_ref[:, here] = image
        products = [residual * residual, direction * image, residual * image, image * image]
        for n, product in enumerate(products):
            for lane in range(0, tile, 128):
                sums[n] += product[:, lane : lane + 128]
    row = jnp.sum(jnp.concatenate(sums, axis=0).T, axis=0, keepdims=True)
    for to in range(16):
        stats_ref[to] = row


def step_kernel(
    stats_ref, solution_ref, residual_ref, direction_ref, image_ref, out0, out1, out2, held, sems
):
    stats = stats_ref[0]
    for source in range(1, 32):
        stats += stats_ref[source]
    norm_now, curvature, cross, square = [stats[:, 64 * n : 64 * n + 64] for n in range(4)]
    step_size = norm_now / curvature
    norm_next = jnp.maximum(norm_now + step_size * (step_size * square - 2.0 * cross), 0.0)
    ratio = norm_next / norm_now
    rows = jnp.concatenate([step_size, ratio], axis=1)
    columns = jnp.broadcast_to(rows, (128, 128)).T
    step_size, ratio = columns[0:64, 0:1], columns[64:128, 0:1]
    outs = (out0, out1, out2)
    copies = []
    for part in range(4):
        here = pl.ds(16 * part, 16)
        step, beta = step_size[16 * part : 16 * part + 16], ratio[16 * part : 16 * part + 16]
        direction = direction_ref[here, :]
        new_residual = residual_ref[here, :] - step * image_ref[here, :]
        held[0, here, :] = solution_ref[here, :] + step * direction
        held[1, here, :] = new_residual
        held[2, here, :] = new_residual + beta * direction
        for n in range(3):
            copy = pltpu.make_async_copy(
                held.at[n, here, :], outs[n].at[here, :], sems.at[3 * part + n]
            )
            copy.start()
            copies.append(copy)
    for copy in copies:
        copy.wait()


def call(kernel, outs, specs, *operands, scratch=(), flops=0, out_spec=VMEM):
    shapes = [jax.ShapeDtypeStruct(shape, dtype) for shape, dtype in outs]
    size = sum(o.size * o.dtype.itemsize for o in operands)
    size += sum(s.size * s.dtype.itemsize for s in shapes)
    single = len(shapes) == 1
    return pl.pallas_call(
        kernel,
        out_shape=shapes[0] if single else shapes,
        in_specs=specs,
        out_specs=out_spec if single else [out_spec] * len(shapes),
        scratch_shapes=list(scratch),
        compiler_params=pltpu.CompilerParams(vmem_limit_bytes=32 * 2**20),
        cost_estimate=pl.CostEstimate(flops=flops, bytes_accessed=size, transcendentals=0),
    )(*operands)


def meets(mine):
    apart = jnp.bitwise_xor(jnp.arange(16, dtype=jnp.int32)[:, None], mine)
    low = jnp.left_shift(1, jnp.arange(4, dtype=jnp.int32))[None, :]
    return (apart >= low) & (apart < 2 * low)


def local(
    features, lengthscale, signal_var, noise_var, factors, gains, solution, residual, direction
):
    core = lax.axis_index("core")
    place = core.astype(jnp.int32).reshape(1)

    projection = jnp.einsum(
        "cp,lpr->lcr", direction.astype(BF), factors, preferred_element_type=F32
    ).astype(BF)
    near_meets = meets(lax.axis_index(CHIP)).reshape(16, 1, 4, 1, 1)
    far_meets = meets(lax.axis_index("z")).reshape(16, 4, 1, 1)
    near = projection[:4].reshape(4, 2, 32, 128).transpose(1, 0, 2, 3)[None]
    near = jnp.sum(jnp.where(near_meets, near, 0.0).astype(F32), axis=2).astype(BF)
    far = projection[4:].reshape(4, 2, 32, 128).transpose(2, 0, 1, 3)
    sent = jnp.concatenate([near.reshape(32, 32, 128), far.reshape(32, 8, 128)], axis=1)
    got = lax.all_to_all(sent, LEAF, 0, 0, tiled=True)

    own = jnp.concatenate([features] + parts_of(lax.optimization_barrier(direction), 2), axis=0)
    other = lax.ppermute(own, "core", SWAP)
    rate = (LOG2E / (lengthscale * lengthscale))[:, None]
    leaf = leaf_term(signal_var, rate, own, own)
    got, leaf = lax.optimization_barrier((got, leaf))
    leaf = leaf_term(signal_var, rate, own, other, leaf)

    plane_sum = jnp.sum(got[:, 32:].astype(F32), axis=0).reshape(1, 4, 2, 128)
    far = jnp.sum(jnp.where(far_meets, plane_sum, 0.0), axis=1).astype(BF)
    far = lax.all_to_all(far, "z", 0, 0, tiled=True)

    near = jnp.sum(got[:, :32].astype(F32).reshape(16, 2, 1, 32, 128), axis=1)
    near = jnp.sum(jnp.where(near_meets.reshape(16, 4, 1, 1), near, 0.0), axis=0)
    near = (gains[:4, None, :] * near).astype(BF)
    near_other = lax.ppermute(near, "core", SWAP)

    far = jnp.sum(jnp.where(far_meets, far.astype(F32)[:, None], 0.0), axis=0)
    far = (gains[4:, None, :] * far).astype(BF).reshape(1, 8, 128)
    far = lax.all_to_all(jnp.broadcast_to(far, (32, 8, 128)), LEAF, 0, 0, tiled=True)
    far = far.reshape(32, 4, 2, 128).transpose(1, 2, 0, 3).reshape(4, 64, 128)

    image, stats = call(
        image_kernel, [((64, 1024), F32), ((16, 1, 256), F32)],
        [SMEM, SMEM] + [VMEM] * 7,
        place, noise_var, near, near_other, far, factors, leaf, direction, residual, flops=2**27,
    )
    stats = lax.all_to_all(stats, CHIP, 0, 0, tiled=True).sum(0)
    stats = jnp.broadcast_to(stats[None], (32, 1, 256))
    stats = lax.all_to_all(stats, ("core", "z"), 0, 0, tiled=True)
    return call(
        step_kernel, [(direction.shape, F32)] * 3, [VMEM] * 5,
        stats, solution, residual, direction, image,
        scratch=[pltpu.VMEM((3,) + direction.shape, F32), pltpu.SemaphoreType.DMA((12,))],
        out_spec=HBM,
    )


def solution(mesh):
    fine = Mesh(mesh.devices.reshape(4, 4, 2, 16), ("x", "y", "core", "z"))
    points = P(None, ("z", "x", "y", "core"))
    return jax.shard_map(
        local,
        mesh=fine,
        in_specs=(
            points,
            P(),
            P(),
            P(),
            P(None, ("z", "x", "y", "core"), None),
            P(),
            points,
            points,
            points,
        ),
        out_specs=(points, points, points),
        check_vma=False,
    )
```

time: 95.4 us -> 92.1 us (0.965)
  other arithmetic: 5.8 us -> 1.62 us
  Pallas kernels: 3.67 us -> 7.23 us
  waiting for transfers between devices: 17.8 us -> 16 us
  matrix products: 3.38 us -> 2.2 us
    pallas_call x0 -> x2, Pallas kernels: none -> 2.19 us  [call(): pl.pallas_call(kernel, out_shape=shapes[0] if single else shapes, in_spec...]
    all_to_all x1, waiting for transfers between devices: 5.98 us -> 3.9 us  [local(): got = lax.all_to_all(sent, LEAF, 0, 0, tiled=True)]
    add x1 -> x0, other arithmetic: 1.96 us -> none  [local(): new_direction = new_residual + (norm_next / norm_now)[:, None] * direction]
    pallas_call x1 -> x2, Pallas kernels: 3.67 us -> 5.05 us  [leaf_term(): pl.pallas_call(leaf_kernel, out_shape=jax.ShapeDtypeStruct((64, own.shape...]
    dot_general x6 -> x1, matrix products: 3.38 us -> 2.2 us  [local(): jnp.einsum('cp,lpr->lcr', direction.astype(BF), factors, preferred_elemen...]
    convert_element_type x1, other arithmetic: 1.2 us -> 0.03 us  [parts_of(): part = value.astype(BF)]
  transfers between devices with their start and end apart: 5 -> 5, of which waited for: 3 -> 3; matrix products, arithmetic and copies ran while one was open for 3% -> 2% of each run, Pallas kernels for 4% -> 6%
where the time goes in v2:
time: 92.1 us; the launch traced here: 91.5 us
  starting transfers between devices  32.8 us (36%)
  blocking collectives  26.7 us (29%)
  waiting for transfers between devices  16 us (17%)
  Pallas kernels  7.23 us (8%)
  local copies, waits for them, and re-layouts  2.69 us (3%)
  between operations  2.24 us (2%)
  matrix products  2.2 us (2%)
  other arithmetic  1.62 us (2%)
    all_to_all x1, blocking collectives, local(): stats = lax.all_to_all(stats, ('core', 'z'), 0, 0, tiled=True)  17 us
    all_to_all x1, starting transfers between devices, local(): far = lax.all_to_all(far, 'z', 0, 0, tiled=True)  13 us
    all_to_all x1, starting transfers between devices, local(): got = lax.all_to_all(sent, LEAF, 0, 0, tiled=True)  10.4 us
    all_to_all x1, blocking collectives, local(): stats = lax.all_to_all(stats, CHIP, 0, 0, tiled=True).sum(0)  9.77 us
    all_to_all x1, waiting for transfers between devices, local(): far = lax.all_to_all(far, 'z', 0, 0, tiled=True)  8.85 us
    pallas_call x2, Pallas kernels, leaf_term(): pl.pallas_call(leaf_kernel, out_shape=jax.ShapeDtypeStruct((64, own.shape...  5.05 us
    all_to_all x1, starting transfers between devices, local(): lax.all_to_all(jnp.broadcast_to(far, (32, 8, 128)), LEAF, 0, 0, tiled=True)  5 us
    all_to_all x1, waiting for transfers between devices, local(): got = lax.all_to_all(sent, LEAF, 0, 0, tiled=True)  3.9 us
  transfers between devices with their start and end apart: 5, of which 3 were waited for; matrix products, arithmetic and copies ran while one was open for 2% of the time, Pallas kernels for 6%

profile of v2, /device:TPU:1, one launch (start us, length us, event | category | flops | bytes accessed | tf_op | source)
XLA Modules:
  0.0 91.5 jit_solution(11094957506398604949)
XLA Ops:
  0.7 0.1 compare_and_fusion
  0.7 0.1 copy.37
  0.8 2.2 %fusion = bf16[8,64,128]{2,1,0:T(8,128)(2,1)S(1)} fusion(bf16[8,1024,128]{2,1,0:T(8,128)(2,1)} %factors_ref.1, f32[64,1024]{1,0:T(8,128)} %direction_ref.3), kind=kOutput, calls=%fused_computation.1 | convolution fusion | flops 134348800 | bytes 2490368 | tf_op jit(solution)/shard_map/cp,lpr->lcr/dot_general | solution.py:183
  3.1 0.1 copy.40
  3.1 0.3 select_reduce_fusion.1
  3.4 0.8 pad_maximum_fusion.1
  4.2 10.4 %all-to-all-start = ((bf16[32,40,128]{2,1,0:T(8,128)(2,1)}), bf16[32,40,128]{2,1,0:T(8,128)(2,1)S(1)}, u32[]{:S(2)}, u32[]{:S(2)}) async-start(bf16[32,40,128]{2,1,0:T(8,128)(2,1)} %pad_maximum_fusion.1), calls=%async_computation | async-start | bytes 655360 | tf_op jit(solution)/shard_map/all_to_all | solution.py:192
  14.7 2.3 %collective-permute-start.1 = (bf16[192,1024]{1,0:T(8,128)(2,1)S(1)}, bf16[192,1024]{1,0:T(8,128)(2,1)}, u32[]{:S(2)}, u32[]{:S(2)}) collective-permute-start(bf16[192,1024]{1,0:T(8,128)(2,1)S(1)} %pad_maximum_fusion.own_ref.other_ref), channel_id=1, source_target_pairs={{0,16},{16,0},{1,17},{17,1},{2,18},{18,2},{3,19},{19,3},{4,20},{20... | collective-permute-start | bytes 1179656 | tf_op jit(solution)/shard_map/ppermute | solution.py:195
  17.0 0.1 copy.41.rate_ref
  18.4 0.0 copy-start.7
  18.4 2.0 %shard_map.112.refs_0_ = f32[64,1024]{1,0:T(8,128)S(1)} custom-call(f32[1]{0:T(128)S(6)} %copy.49.signal_ref, f32[64,1]{1,0:T(8,128)S(1)} %copy.41.rate_ref, bf16[192,1024]{1,0:T(8,128)(2,1)S(1)} %pad_maximum_fusion.own_ref.other_ref, bf16[192,1024]{1,0:T(8,128)(2,1)S(1)} %pad_maximum_fusion.own_ref.other_ref), custom_call_target="tpu_custom_call" | custom-call | flops 1610612736 | bytes 1048576 | tf_op jit(solution)/shard_map/pallas_call | solution.py:66
  20.4 0.0 copy-start.4
  20.5 3.9 %all-to-all-done = bf16[32,40,128]{2,1,0:T(8,128)(2,1)S(1)} async-done(((bf16[32,40,128]{2,1,0:T(8,128)(2,1)}), bf16[32,40,128]{2,1,0:T(8,128)(2,1)S(1)}, u32[]{:S(2)}, u32[]{:S(2)}) %all-to-all-start) | async-done | bytes 327712 | tf_op jit(solution)/shard_map/all_to_all | solution.py:192
  24.4 0.1 select_reduce_fusion.3
  24.5 0.6 copy.42
  25.1 13.0 %all-to-all-start.1 = ((bf16[16,2,128]{2,1,0:T(2,128)(2,1)}), bf16[16,2,128]{2,1,0:T(2,128)(2,1)S(1)}, u32[]{:S(2)}, u32[]{:S(2)}) async-start(bf16[16,2,128]{2,1,0:T(2,128)(2,1)} %copy.42), calls=%async_computation.1 | async-start | bytes 16384 | tf_op jit(solution)/shard_map/all_to_all | solution.py:203
  38.1 0.1 select_reduce_fusion
  38.3 2.2 %collective-permute-start = (bf16[4,32,128]{2,1,0:T(8,128)(2,1)S(1)}, bf16[4,32,128]{2,1,0:T(8,128)(2,1)S(1)}, u32[]{:S(2)}, u32[]{:S(2)}) collective-permute-start(bf16[4,32,128]{2,1,0:T(8,128)(2,1)S(1)} %multiply_convert_fusion.near_ref), channel_id=1, source_target_pairs={{0,16},{16,0},{1,17},{17,1},{2,18},{18,2},{3,19},{19,3},{4,20},{20... | collective-permute-start | bytes 98312 | tf_op jit(solution)/shard_map/ppermute | solution.py:208
  40.5 8.9 %all-to-all-done.1 = bf16[16,2,128]{2,1,0:T(2,128)(2,1)S(1)} async-done(((bf16[16,2,128]{2,1,0:T(2,128)(2,1)}), bf16[16,2,128]{2,1,0:T(2,128)(2,1)S(1)}, u32[]{:S(2)}, u32[]{:S(2)}) %all-to-all-start.1) | async-done | bytes 8224 | tf_op jit(solution)/shard_map/all_to_all | solution.py:203
  49.4 0.1 select_reduce_fusion.2
  49.5 0.6 broadcast_in_dim.112
  50.1 5.0 %all-to-all-start.2 = ((bf16[32,8,128]{2,1,0:T(8,128)(2,1)}), bf16[32,8,128]{2,1,0:T(8,128)(2,1)S(1)}, u32[]{:S(2)}, u32[]{:S(2)}) async-start(bf16[32,8,128]{2,1,0:T(8,128)(2,1)} %broadcast_in_dim.112), calls=%async_computation.2 | async-start | bytes 131072 | tf_op jit(solution)/shard_map/all_to_all | solution.py:212
  55.1 0.0 copy-start
  55.1 0.0 copy-start.2
  55.2 0.0 copy-start.5
  55.2 1.1 %copy-done.5 = f32[64,1024]{1,0:T(8,128)S(1)} copy-done((f32[64,1024]{1,0:T(8,128)S(1)}, f32[64,1024]{1,0:T(8,128)}, u32[]{:S(2)}) %copy-start.5) | copy-done | bytes 262168
  56.3 3.0 %shard_map.113.leaf_ref = f32[64,1024]{1,0:T(8,128)S(1)} custom-call(f32[1]{0:T(128)S(6)} %copy.49.signal_ref, f32[64,1]{1,0:T(8,128)S(1)} %copy.41.rate_ref, bf16[192,1024]{1,0:T(8,128)(2,1)S(1)} %pad_maximum_fusion.own_ref.other_ref, bf16[192,1024]{1,0:T(8,128)(2,1)} %collective-permute-done.1.other_ref, f32[64,1024]{1,0:T(8,128)S(1)} %copy-done.5), custom_call_target="tpu_custom_call" | custom-call | flops 1610612736 | bytes 1048576 | tf_op jit(solution)/shard_map/pallas_call | solution.py:66
  59.3 3.2 %all-to-all-done.2 = bf16[32,8,128]{2,1,0:T(8,128)(2,1)S(1)} async-done(((bf16[32,8,128]{2,1,0:T(8,128)(2,1)}), bf16[32,8,128]{2,1,0:T(8,128)(2,1)S(1)}, u32[]{:S(2)}, u32[]{:S(2)}) %all-to-all-start.2) | async-done | bytes 65568 | tf_op jit(solution)/shard_map/all_to_all | solution.py:212
  62.6 0.9 shard_map.114
  63.4 9.8 %all_to_all.25 = f32[16,1,256]{2,1,0:T(1,128)S(1)} all-to-all(f32[16,1,256]{2,1,0:T(1,128)S(1)} %get-tuple-element.9), channel_id=1, replica_groups=mesh['x'=4,'y'=4,'core'=2,'z'=16] {'x','y'}, dimensions={0} | all-to-all | bytes 32768 | tf_op jit(solution)/shard_map/all_to_all | solution.py:220
  73.3 17.0 %all_to_all.26.stats_ref = f32[32,1,256]{2,1,0:T(1,128)S(1)} all-to-all(f32[32,1,256]{2,1,0:T(1,128)S(1)} %broadcast_in_dim.113), channel_id=1, replica_groups=mesh['x'=4,'y'=4,'core'=2,'z'=16] {'core','z'}, dimensions={0} | all-to-all | bytes 65536 | tf_op jit(solution)/shard_map/all_to_all | solution.py:222
  90.2 1.3 %shard_map.115 = (f32[64,1024]{1,0:T(8,128)}, f32[64,1024]{1,0:T(8,128)}, f32[64,1024]{1,0:T(8,128)}) custom-call(f32[32,1,256]{2,1,0:T(1,128)S(1)} %all_to_all.26.stats_ref, f32[64,1024]{1,0:T(8,128)S(1)} %copy-done.3, f32[64,1024]{1,0:T(8,128)S(1)} %copy-done.2, f32[64,1024]{1,0:T(8,128)S(1)} %copy-done.1, f32[64,1024]{1,0:T(8,128)S(1)} %get-tuple-element.10.image_ref), custom_call_target="tpu_custom_call" | custom-call | bytes 1867776 | tf_op jit(solution)/shard_map/pallas_call | solution.py:160
  (29 shorter events, 0.3 us)
Async XLA Ops:
  0.8 13.8 %copy-start.1 = (f32[64,1024]{1,0:T(8,128)S(1)}, f32[64,1024]{1,0:T(8,128)}, u32[]{:S(2)}) copy-start(f32[64,1024]{1,0:T(8,128)} %direction_ref.3) | copy-start | bytes 786436
  0.8 13.8 %copy-start.6 = (bf16[64,1024]{1,0:T(8,128)(2,1)S(1)}, bf16[64,1024]{1,0:T(8,128)(2,1)}, u32[]{:S(2)}) copy-start(bf16[64,1024]{1,0:T(8,128)(2,1)} %param.9) | copy-start | bytes 393220
  3.1 13.9 %copy-start.8 = (f32[64]{0:T(128)S(1)}, f32[64]{0:T(128)}, u32[]{:S(2)}) copy-start(f32[64]{0:T(128)} %param.10) | copy-start | bytes 772
  4.2 20.2 %all-to-all-start = ((bf16[32,40,128]{2,1,0:T(8,128)(2,1)}), bf16[32,40,128]{2,1,0:T(8,128)(2,1)S(1)}, u32[]{:S(2)}, u32[]{:S(2)}) async-start(bf16[32,40,128]{2,1,0:T(8,128)(2,1)} %pad_maximum_fusion.1), calls=%async_computation | async-start | bytes 655360 | tf_op jit(solution)/shard_map/all_to_all | solution.py:192
  14.7 40.5 %collective-permute-start.1 = (bf16[192,1024]{1,0:T(8,128)(2,1)S(1)}, bf16[192,1024]{1,0:T(8,128)(2,1)}, u32[]{:S(2)}, u32[]{:S(2)}) collective-permute-start(bf16[192,1024]{1,0:T(8,128)(2,1)S(1)} %pad_maximum_fusion.own_ref.other_ref), channel_id=1, source_target_pairs={{0,16},{16,0},{1,17},{17,1},{2,18},{18,2},{3,19},{19,3},{4,20},{20... | collective-permute-start | bytes 1179656 | tf_op jit(solution)/shard_map/ppermute | solution.py:195
  18.4 2.0 %copy-start.7 = (f32[8,128]{1,0:T(8,128)S(1)}, f32[8,128]{1,0:T(8,128)}, u32[]{:S(2)}) copy-start(f32[8,128]{1,0:T(8,128)} %param.14) | copy-start | bytes 12292
  20.4 29.7 %copy-start.4 = (f32[64,1024]{1,0:T(8,128)}, f32[64,1024]{1,0:T(8,128)S(1)}, u32[]{:S(2)}) copy-start(f32[64,1024]{1,0:T(8,128)S(1)} %shard_map.112.refs_0_) | copy-start | bytes 786436
  25.1 24.2 %all-to-all-start.1 = ((bf16[16,2,128]{2,1,0:T(2,128)(2,1)}), bf16[16,2,128]{2,1,0:T(2,128)(2,1)S(1)}, u32[]{:S(2)}, u32[]{:S(2)}) async-start(bf16[16,2,128]{2,1,0:T(2,128)(2,1)} %copy.42), calls=%async_computation.1 | async-start | bytes 16384 | tf_op jit(solution)/shard_map/all_to_all | solution.py:203
  38.3 24.2 %collective-permute-start = (bf16[4,32,128]{2,1,0:T(8,128)(2,1)S(1)}, bf16[4,32,128]{2,1,0:T(8,128)(2,1)S(1)}, u32[]{:S(2)}, u32[]{:S(2)}) collective-permute-start(bf16[4,32,128]{2,1,0:T(8,128)(2,1)S(1)} %multiply_convert_fusion.near_ref), channel_id=1, source_target_pairs={{0,16},{16,0},{1,17},{17,1},{2,18},{18,2},{3,19},{19,3},{4,20},{20... | collective-permute-start | bytes 98312 | tf_op jit(solution)/shard_map/ppermute | solution.py:208
  50.1 12.4 %all-to-all-start.2 = ((bf16[32,8,128]{2,1,0:T(8,128)(2,1)}), bf16[32,8,128]{2,1,0:T(8,128)(2,1)S(1)}, u32[]{:S(2)}, u32[]{:S(2)}) async-start(bf16[32,8,128]{2,1,0:T(8,128)(2,1)} %broadcast_in_dim.112), calls=%async_computation.2 | async-start | bytes 131072 | tf_op jit(solution)/shard_map/all_to_all | solution.py:212
  55.1 7.4 %copy-start = (bf16[8,1024,128]{2,1,0:T(8,128)(2,1)S(1)}, bf16[8,1024,128]{2,1,0:T(8,128)(2,1)}, u32[]{:S(2)}) copy-start(bf16[8,1024,128]{2,1,0:T(8,128)(2,1)} %factors_ref.1) | copy-start | bytes 6291460
  55.1 7.4 %copy-start.2 = (f32[64,1024]{1,0:T(8,128)S(1)}, f32[64,1024]{1,0:T(8,128)}, u32[]{:S(2)}) copy-start(f32[64,1024]{1,0:T(8,128)} %residual_ref.3) | copy-start | bytes 786436
  55.2 1.1 %copy-start.5 = (f32[64,1024]{1,0:T(8,128)S(1)}, f32[64,1024]{1,0:T(8,128)}, u32[]{:S(2)}) copy-start(f32[64,1024]{1,0:T(8,128)} %copy-done.4) | copy-start | bytes 786436
  59.3 30.9 %copy-start.3 = (f32[64,1024]{1,0:T(8,128)S(1)}, f32[64,1024]{1,0:T(8,128)}, u32[]{:S(2)}) copy-start(f32[64,1024]{1,0:T(8,128)} %solution_ref.1) | copy-start | bytes 786436

commit v3 on v2

--- a/solution.py
+++ b/solution.py
@@ -14,6 +14,11 @@
 SMEM = pl.BlockSpec(memory_space=pltpu.SMEM)
 HBM = pl.BlockSpec(memory_space=pltpu.HBM)
 SWAP = [(0, 1), (1, 0)]
+PLANES = [8, 0, 15, 1, 14, 2, 13, 3, 12, 4, 11, 5, 10, 6, 9, 7]
+COLUMN = [24, 16, 31, 17, 30, 18, 29, 19, 28, 20, 27, 21, 26, 22, 25, 23, 8, 0, 15, 1, 14, 2, 13, 3, 12, 4, 11, 5, 10, 6, 9, 7]
+CHIPS = [15, 14, 13, 12, 11, 10, 9, 8, 7, 6, 5, 4, 3, 2, 1, 0]
+LEAVES = [30, 31, 28, 29, 26, 27, 24, 25, 22, 23, 20, 21, 18, 19, 16, 17, 14, 15, 12, 13, 10, 11, 8, 9, 6, 7, 4, 5, 2, 3, 0, 1]
+SQUARE = [15, 14, 13, 12, 11, 10, 9, 8, 7, 6, 5, 4, 3, 2, 1, 0]
 BF = jnp.bfloat16
 F32 = jnp.float32
 
@@ -168,8 +173,8 @@
     )(*operands)
 
 
-def meets(mine):
-    apart = jnp.bitwise_xor(jnp.arange(16, dtype=jnp.int32)[:, None], mine)
+def meets(mine, order):
+    apart = jnp.bitwise_xor(jnp.array(order, dtype=jnp.int32)[:, None], mine)
     low = jnp.left_shift(1, jnp.arange(4, dtype=jnp.int32))[None, :]
     return (apart >= low) & (apart < 2 * low)
 
@@ -183,13 +188,13 @@
     projection = jnp.einsum(
         "cp,lpr->lcr", direction.astype(BF), factors, preferred_element_type=F32
     ).astype(BF)
-    near_meets = meets(lax.axis_index(CHIP)).reshape(16, 1, 4, 1, 1)
-    far_meets = meets(lax.axis_index("z")).reshape(16, 4, 1, 1)
+    near_meets = meets(lax.axis_index(CHIP), CHIPS).reshape(16, 1, 4, 1, 1)
+    far_meets = meets(lax.axis_index("z"), PLANES).reshape(16, 4, 1, 1)
     near = projection[:4].reshape(4, 2, 32, 128).transpose(1, 0, 2, 3)[None]
     near = jnp.sum(jnp.where(near_meets, near, 0.0).astype(F32), axis=2).astype(BF)
     far = projection[4:].reshape(4, 2, 32, 128).transpose(2, 0, 1, 3)
     sent = jnp.concatenate([near.reshape(32, 32, 128), far.reshape(32, 8, 128)], axis=1)
-    got = lax.all_to_all(sent, LEAF, 0, 0, tiled=True)
+    got = lax.all_to_all(sent, LEAF, 0, 0, tiled=True, axis_index_groups=[LEAVES])
 
     own = jnp.concatenate([features] + parts_of(lax.optimization_barrier(direction), 2), axis=0)
     other = lax.ppermute(own, "core", SWAP)
@@ -200,7 +205,7 @@
 
     plane_sum = jnp.sum(got[:, 32:].astype(F32), axis=0).reshape(1, 4, 2, 128)
     far = jnp.sum(jnp.where(far_meets, plane_sum, 0.0), axis=1).astype(BF)
-    far = lax.all_to_all(far, "z", 0, 0, tiled=True)
+    far = lax.all_to_all(far, "z", 0, 0, tiled=True, axis_index_groups=[PLANES])
 
     near = jnp.sum(got[:, :32].astype(F32).reshape(16, 2, 1, 32, 128), axis=1)
     near = jnp.sum(jnp.where(near_meets.reshape(16, 4, 1, 1), near, 0.0), axis=0)
@@ -209,7 +214,7 @@
 
     far = jnp.sum(jnp.where(far_meets, far.astype(F32)[:, None], 0.0), axis=0)
     far = (gains[4:, None, :] * far).astype(BF).reshape(1, 8, 128)
-    far = lax.all_to_all(jnp.broadcast_to(far, (32, 8, 128)), LEAF, 0, 0, tiled=True)
+    far = lax.all_to_all(jnp.broadcast_to(far, (32, 8, 128)), LEAF, 0, 0, tiled=True, axis_index_groups=[LEAVES])
     far = far.reshape(32, 4, 2, 128).transpose(1, 2, 0, 3).reshape(4, 64, 128)
 
     image, stats = call(
@@ -217,9 +222,9 @@
         [SMEM, SMEM] + [VMEM] * 7,
         place, noise_var, near, near_other, far, factors, leaf, direction, residual, flops=2**27,
     )
-    stats = lax.all_to_all(stats, CHIP, 0, 0, tiled=True).sum(0)
+    stats = lax.all_to_all(stats, CHIP, 0, 0, tiled=True, axis_index_groups=[SQUARE]).sum(0)
     stats = jnp.broadcast_to(stats[None], (32, 1, 256))
-    stats = lax.all_to_all(stats, ("core", "z"), 0, 0, tiled=True)
+    stats = lax.all_to_all(stats, ("core", "z"), 0, 0, tiled=True, axis_index_groups=[COLUMN])
     return call(
         step_kernel, [(direction.shape, F32)] * 3, [VMEM] * 5,
         stats, solution, residual, direction, image,

time: 92.1 us -> 83.5 us (0.907)
  waiting for transfers between devices: 16 us -> 0.59 us
  starting transfers between devices: 32.8 us -> 40.2 us
  blocking collectives: 26.7 us -> 25.5 us
    all_to_all x3, waiting for transfers between devices: 16 us -> 0.58 us  [the longest x1 0.58 us: local(): lax.all_to_all(sent, LEAF, 0, 0, tiled=True, axis_index_groups=[LEAVES])]
    all_to_all x3, starting transfers between devices: 28.4 us -> 35.5 us  [the longest x1 14.9 us: local(): far = lax.all_to_all(far, 'z', 0, 0, tiled=True, axis_index_groups=[PLANES])]
    all_to_all x2, blocking collectives: 26.7 us -> 25.5 us  [the longest x1 15.9 us: local(): lax.all_to_all(stats, ('core', 'z'), 0, 0, tiled=True, axis_index_groups=...]
  transfers between devices with their start and end apart: 5 -> 5, of which waited for: 3 -> 1; matrix products, arithmetic and copies ran while one was open for 2% -> 2% of each run, Pallas kernels for 6% -> 6%
where the time goes in v3:
time: 83.5 us; the launch traced here: 83 us
  starting transfers between devices  40.2 us (48%)
  blocking collectives  25.5 us (31%)
  Pallas kernels  7.23 us (9%)
  local copies, waits for them, and re-layouts  2.69 us (3%)
  other arithmetic  2.29 us (3%)
  between operations  2.25 us (3%)
  matrix products  2.2 us (3%)
    all_to_all x1, blocking collectives, local(): lax.all_to_all(stats, ('core', 'z'), 0, 0, tiled=True, axis_index_groups=...  15.9 us
    all_to_all x1, starting transfers between devices, local(): far = lax.all_to_all(far, 'z', 0, 0, tiled=True, axis_index_groups=[PLANES])  14.9 us
    all_to_all x1, starting transfers between devices, local(): lax.all_to_all(sent, LEAF, 0, 0, tiled=True, axis_index_groups=[LEAVES])  13.4 us
    all_to_all x1, blocking collectives, local(): lax.all_to_all(stats, CHIP, 0, 0, tiled=True, axis_index_groups=[SQUARE])  9.64 us
    all_to_all x1, starting transfers between devices, local(): lax.all_to_all(jnp.broadcast_to(far, (32, 8, 128)), LEAF, 0, 0, tiled=Tru...  7.22 us
    pallas_call x2, Pallas kernels, leaf_term(): pl.pallas_call(leaf_kernel, out_shape=jax.ShapeDtypeStruct((64, own.shape...  5.05 us
    ppermute x1, starting transfers between devices, local(): near_other = lax.ppermute(near, 'core', SWAP)  2.4 us
    ppermute x1, starting transfers between devices, local(): other = lax.ppermute(own, 'core', SWAP)  2.27 us
  transfers between devices with their start and end apart: 5, of which 1 were waited for; matrix products, arithmetic and copies ran while one was open for 2% of the time, Pallas kernels for 6%

profile of v3, /device:TPU:1, one launch (start us, length us, event | category | flops | bytes accessed | tf_op | source)
XLA Modules:
  0.0 83.0 jit_solution(15053362031330658951)
XLA Ops:
  0.7 0.7 broadcast_xor_fusion
  1.3 0.1 compare_and_fusion
  1.4 0.1 copy.39
  1.5 2.2 %fusion = bf16[8,64,128]{2,1,0:T(8,128)(2,1)S(1)} fusion(bf16[8,1024,128]{2,1,0:T(8,128)(2,1)} %factors_ref.1, f32[64,1024]{1,0:T(8,128)} %direction_ref.3), kind=kOutput, calls=%fused_computation.1 | convolution fusion | flops 134348800 | bytes 2490368 | tf_op jit(solution)/shard_map/cp,lpr->lcr/dot_general | solution.py:188
  3.7 0.0 copy-start.8
  3.8 0.1 copy.42
  3.8 0.3 select_reduce_fusion.1
  4.1 0.8 pad_maximum_fusion.1
  4.9 13.4 %all-to-all-start = ((bf16[32,40,128]{2,1,0:T(8,128)(2,1)}), bf16[32,40,128]{2,1,0:T(8,128)(2,1)S(1)}, u32[]{:S(2)}, u32[]{:S(2)}) async-start(bf16[32,40,128]{2,1,0:T(8,128)(2,1)} %pad_maximum_fusion.1), calls=%async_computation | async-start | bytes 655360 | tf_op jit(solution)/shard_map/all_to_all | solution.py:197
  18.3 2.3 %collective-permute-start.1 = (bf16[192,1024]{1,0:T(8,128)(2,1)S(1)}, bf16[192,1024]{1,0:T(8,128)(2,1)}, u32[]{:S(2)}, u32[]{:S(2)}) collective-permute-start(bf16[192,1024]{1,0:T(8,128)(2,1)S(1)} %pad_maximum_fusion.own_ref.other_ref), channel_id=1, source_target_pairs={{0,16},{16,0},{1,17},{17,1},{2,18},{18,2},{3,19},{19,3},{4,20},{20... | collective-permute-start | bytes 1179656 | tf_op jit(solution)/shard_map/ppermute | solution.py:200
  20.6 0.1 copy.43.rate_ref
  22.0 0.0 copy-start.7
  22.0 2.0 %shard_map.130.refs_0_ = f32[64,1024]{1,0:T(8,128)S(1)} custom-call(f32[1]{0:T(128)S(6)} %copy.51.signal_ref, f32[64,1]{1,0:T(8,128)S(1)} %copy.43.rate_ref, bf16[192,1024]{1,0:T(8,128)(2,1)S(1)} %pad_maximum_fusion.own_ref.other_ref, bf16[192,1024]{1,0:T(8,128)(2,1)S(1)} %pad_maximum_fusion.own_ref.other_ref), custom_call_target="tpu_custom_call" | custom-call | flops 1610612736 | bytes 1048576 | tf_op jit(solution)/shard_map/pallas_call | solution.py:71
  24.1 0.0 copy-start.4
  24.1 0.6 all-to-all-done
  24.8 0.1 select_reduce_fusion.3
  24.8 0.6 copy.44
  25.5 14.9 %all-to-all-start.1 = ((bf16[16,2,128]{2,1,0:T(2,128)(2,1)}), bf16[16,2,128]{2,1,0:T(2,128)(2,1)S(1)}, u32[]{:S(2)}, u32[]{:S(2)}) async-start(bf16[16,2,128]{2,1,0:T(2,128)(2,1)} %copy.44), calls=%async_computation.1 | async-start | bytes 16384 | tf_op jit(solution)/shard_map/all_to_all | solution.py:208
  40.4 0.1 select_reduce_fusion
  40.6 2.4 %collective-permute-start = (bf16[4,32,128]{2,1,0:T(8,128)(2,1)S(1)}, bf16[4,32,128]{2,1,0:T(8,128)(2,1)S(1)}, u32[]{:S(2)}, u32[]{:S(2)}) collective-permute-start(bf16[4,32,128]{2,1,0:T(8,128)(2,1)S(1)} %multiply_convert_fusion.near_ref), channel_id=1, source_target_pairs={{0,16},{16,0},{1,17},{17,1},{2,18},{18,2},{3,19},{19,3},{4,20},{20... | collective-permute-start | bytes 98312 | tf_op jit(solution)/shard_map/ppermute | solution.py:213
  43.0 0.1 select_reduce_fusion.2
  43.1 0.6 broadcast_in_dim.112
  43.7 7.2 %all-to-all-start.2 = ((bf16[32,8,128]{2,1,0:T(8,128)(2,1)}), bf16[32,8,128]{2,1,0:T(8,128)(2,1)S(1)}, u32[]{:S(2)}, u32[]{:S(2)}) async-start(bf16[32,8,128]{2,1,0:T(8,128)(2,1)} %broadcast_in_dim.112), calls=%async_computation.2 | async-start | bytes 131072 | tf_op jit(solution)/shard_map/all_to_all | solution.py:217
  51.0 0.0 copy-start
  51.0 0.0 copy-start.5
  51.0 1.1 %copy-done.5 = f32[64,1024]{1,0:T(8,128)S(1)} copy-done((f32[64,1024]{1,0:T(8,128)S(1)}, f32[64,1024]{1,0:T(8,128)}, u32[]{:S(2)}) %copy-start.5) | copy-done | bytes 262168
  52.1 3.0 %shard_map.131.leaf_ref = f32[64,1024]{1,0:T(8,128)S(1)} custom-call(f32[1]{0:T(128)S(6)} %copy.51.signal_ref, f32[64,1]{1,0:T(8,128)S(1)} %copy.43.rate_ref, bf16[192,1024]{1,0:T(8,128)(2,1)S(1)} %pad_maximum_fusion.own_ref.other_ref, bf16[192,1024]{1,0:T(8,128)(2,1)} %collective-permute-done.1.other_ref, f32[64,1024]{1,0:T(8,128)S(1)} %copy-done.5), custom_call_target="tpu_custom_call" | custom-call | flops 1610612736 | bytes 1048576 | tf_op jit(solution)/shard_map/pallas_call | solution.py:71
  55.1 0.0 copy-start.3
  55.2 0.9 %shard_map.132 = (f32[64,1024]{1,0:T(8,128)S(1)}, f32[16,1,256]{2,1,0:T(1,128)S(1)}) custom-call(s32[1]{0:T(128)} %bitcast.place_ref, f32[1]{0:T(128)S(6)} %copy.52.noise_ref, bf16[4,32,128]{2,1,0:T(8,128)(2,1)S(1)} %multiply_convert_fusion.near_ref, bf16[4,32,128]{2,1,0:T(8,128)(2,1)S(1)} %collective-permute-done.near_other_ref, ...), custom_call_target="tpu_custom_call" | custom-call | flops 134217728 | bytes 3293192 | tf_op jit(solution)/shard_map/pallas_call | solution.py:165
  56.1 9.6 %all_to_all.25 = f32[16,1,256]{2,1,0:T(1,128)S(1)} all-to-all(f32[16,1,256]{2,1,0:T(1,128)S(1)} %get-tuple-element.9), channel_id=1, replica_groups={{480,448,416,384,352,320,288,256,224,192,160,128,96,64,32,0},{481,449,4..., dimensions={0} | all-to-all | bytes 32768 | tf_op jit(solution)/shard_map/all_to_all | solution.py:225
  65.8 15.9 %all_to_all.26.stats_ref = f32[32,1,256]{2,1,0:T(1,128)S(1)} all-to-all(f32[32,1,256]{2,1,0:T(1,128)S(1)} %broadcast_in_dim.113), channel_id=1, replica_groups={{24,16,31,17,30,18,29,19,28,20,27,21,26,22,25,23,8,0,15,1,14,2,13,3,12,..., dimensions={0} | all-to-all | bytes 65536 | tf_op jit(solution)/shard_map/all_to_all | solution.py:227
  81.7 1.3 %shard_map.133 = (f32[64,1024]{1,0:T(8,128)}, f32[64,1024]{1,0:T(8,128)}, f32[64,1024]{1,0:T(8,128)}) custom-call(f32[32,1,256]{2,1,0:T(1,128)S(1)} %all_to_all.26.stats_ref, f32[64,1024]{1,0:T(8,128)S(1)} %copy-done.3, f32[64,1024]{1,0:T(8,128)S(1)} %copy-done.2, f32[64,1024]{1,0:T(8,128)S(1)} %copy-done.1, f32[64,1024]{1,0:T(8,128)S(1)} %get-tuple-element.10.image_ref), custom_call_target="tpu_custom_call" | custom-call | bytes 1867776 | tf_op jit(solution)/shard_map/pallas_call | solution.py:165
  (29 shorter events, 0.3 us)
Async XLA Ops:
  1.5 16.7 %copy-start.1 = (f32[64,1024]{1,0:T(8,128)S(1)}, f32[64,1024]{1,0:T(8,128)}, u32[]{:S(2)}) copy-start(f32[64,1024]{1,0:T(8,128)} %direction_ref.3) | copy-start | bytes 786436
  1.5 16.8 %copy-start.6 = (bf16[64,1024]{1,0:T(8,128)(2,1)S(1)}, bf16[64,1024]{1,0:T(8,128)(2,1)}, u32[]{:S(2)}) copy-start(bf16[64,1024]{1,0:T(8,128)(2,1)} %param.11) | copy-start | bytes 393220
  3.7 16.9 %copy-start.8 = (f32[64]{0:T(128)S(1)}, f32[64]{0:T(128)}, u32[]{:S(2)}) copy-start(f32[64]{0:T(128)} %param.12) | copy-start | bytes 772
  4.9 19.8 %all-to-all-start = ((bf16[32,40,128]{2,1,0:T(8,128)(2,1)}), bf16[32,40,128]{2,1,0:T(8,128)(2,1)S(1)}, u32[]{:S(2)}, u32[]{:S(2)}) async-start(bf16[32,40,128]{2,1,0:T(8,128)(2,1)} %pad_maximum_fusion.1), calls=%async_computation | async-start | bytes 655360 | tf_op jit(solution)/shard_map/all_to_all | solution.py:197
  18.3 32.7 %collective-permute-start.1 = (bf16[192,1024]{1,0:T(8,128)(2,1)S(1)}, bf16[192,1024]{1,0:T(8,128)(2,1)}, u32[]{:S(2)}, u32[]{:S(2)}) collective-permute-start(bf16[192,1024]{1,0:T(8,128)(2,1)S(1)} %pad_maximum_fusion.own_ref.other_ref), channel_id=1, source_target_pairs={{0,16},{16,0},{1,17},{17,1},{2,18},{18,2},{3,19},{19,3},{4,20},{20... | collective-permute-start | bytes 1179656 | tf_op jit(solution)/shard_map/ppermute | solution.py:200
  22.0 2.0 %copy-start.7 = (f32[8,128]{1,0:T(8,128)S(1)}, f32[8,128]{1,0:T(8,128)}, u32[]{:S(2)}) copy-start(f32[8,128]{1,0:T(8,128)} %param.16) | copy-start | bytes 12292
  24.1 19.6 %copy-start.4 = (f32[64,1024]{1,0:T(8,128)}, f32[64,1024]{1,0:T(8,128)S(1)}, u32[]{:S(2)}) copy-start(f32[64,1024]{1,0:T(8,128)S(1)} %shard_map.130.refs_0_) | copy-start | bytes 786436
  25.5 17.5 %all-to-all-start.1 = ((bf16[16,2,128]{2,1,0:T(2,128)(2,1)}), bf16[16,2,128]{2,1,0:T(2,128)(2,1)S(1)}, u32[]{:S(2)}, u32[]{:S(2)}) async-start(bf16[16,2,128]{2,1,0:T(2,128)(2,1)} %copy.44), calls=%async_computation.1 | async-start | bytes 16384 | tf_op jit(solution)/shard_map/all_to_all | solution.py:208
  40.6 14.6 %collective-permute-start = (bf16[4,32,128]{2,1,0:T(8,128)(2,1)S(1)}, bf16[4,32,128]{2,1,0:T(8,128)(2,1)S(1)}, u32[]{:S(2)}, u32[]{:S(2)}) collective-permute-start(bf16[4,32,128]{2,1,0:T(8,128)(2,1)S(1)} %multiply_convert_fusion.near_ref), channel_id=1, source_target_pairs={{0,16},{16,0},{1,17},{17,1},{2,18},{18,2},{3,19},{19,3},{4,20},{20... | collective-permute-start | bytes 98312 | tf_op jit(solution)/shard_map/ppermute | solution.py:213
  43.7 11.4 %all-to-all-start.2 = ((bf16[32,8,128]{2,1,0:T(8,128)(2,1)}), bf16[32,8,128]{2,1,0:T(8,128)(2,1)S(1)}, u32[]{:S(2)}, u32[]{:S(2)}) async-start(bf16[32,8,128]{2,1,0:T(8,128)(2,1)} %broadcast_in_dim.112), calls=%async_computation.2 | async-start | bytes 131072 | tf_op jit(solution)/shard_map/all_to_all | solution.py:217
  51.0 4.2 %copy-start = (bf16[8,1024,128]{2,1,0:T(8,128)(2,1)S(1)}, bf16[8,1024,128]{2,1,0:T(8,128)(2,1)}, u32[]{:S(2)}) copy-start(bf16[8,1024,128]{2,1,0:T(8,128)(2,1)} %factors_ref.1) | copy-start | bytes 6291460
  51.0 4.2 %copy-start.2 = (f32[64,1024]{1,0:T(8,128)S(1)}, f32[64,1024]{1,0:T(8,128)}, u32[]{:S(2)}) copy-start(f32[64,1024]{1,0:T(8,128)} %residual_ref.3) | copy-start | bytes 786436
  51.0 1.1 %copy-start.5 = (f32[64,1024]{1,0:T(8,128)S(1)}, f32[64,1024]{1,0:T(8,128)}, u32[]{:S(2)}) copy-start(f32[64,1024]{1,0:T(8,128)} %copy-done.4) | copy-start | bytes 786436
  55.1 26.5 %copy-start.3 = (f32[64,1024]{1,0:T(8,128)S(1)}, f32[64,1024]{1,0:T(8,128)}, u32[]{:S(2)}) copy-start(f32[64,1024]{1,0:T(8,128)} %solution_ref.1) | copy-start | bytes 786436

commit v4 on v3

--- a/solution.py
+++ b/solution.py
@@ -14,11 +14,10 @@
 SMEM = pl.BlockSpec(memory_space=pltpu.SMEM)
 HBM = pl.BlockSpec(memory_space=pltpu.HBM)
 SWAP = [(0, 1), (1, 0)]
-PLANES = [8, 0, 15, 1, 14, 2, 13, 3, 12, 4, 11, 5, 10, 6, 9, 7]
-COLUMN = [24, 16, 31, 17, 30, 18, 29, 19, 28, 20, 27, 21, 26, 22, 25, 23, 8, 0, 15, 1, 14, 2, 13, 3, 12, 4, 11, 5, 10, 6, 9, 7]
-CHIPS = [15, 14, 13, 12, 11, 10, 9, 8, 7, 6, 5, 4, 3, 2, 1, 0]
-LEAVES = [30, 31, 28, 29, 26, 27, 24, 25, 22, 23, 20, 21, 18, 19, 16, 17, 14, 15, 12, 13, 10, 11, 8, 9, 6, 7, 4, 5, 2, 3, 0, 1]
-SQUARE = [15, 14, 13, 12, 11, 10, 9, 8, 7, 6, 5, 4, 3, 2, 1, 0]
+PLANES = [z ^ 8 for z in range(16)]
+COLUMN = [16 * core + z for core in (1, 0) for z in PLANES]
+LEAVES = [leaf ^ 30 for leaf in range(32)]
+SQUARE = [chip ^ 15 for chip in range(16)]
 BF = jnp.bfloat16
 F32 = jnp.float32
 
@@ -61,7 +60,7 @@
         high, low = parts_of(jnp.exp2(power), 2)
         both = lax.dot_general(high, value, dims, preferred_element_type=F32).T
         rest = lax.dot_general(low, value[0:64], dims, preferred_element_type=F32).T
-        result = signal_ref[0] * (both[0:64] + both[64:128] + rest)
+        result = signal_ref[...] * (both[0:64] + both[64:128] + rest)
         if len(refs) > 1:
             result += refs[0][:, here]
         out_ref[:, here] = result
@@ -71,7 +70,7 @@
     return pl.pallas_call(
         leaf_kernel,
         out_shape=jax.ShapeDtypeStruct((64, own.shape[1]), F32),
-        in_specs=[SMEM] + [VMEM] * (3 + len(base)),
+        in_specs=[VMEM] * (4 + len(base)),
         out_specs=VMEM,
         compiler_params=pltpu.CompilerParams(vmem_limit_bytes=40 * 2**20),
         cost_estimate=pl.CostEstimate(
@@ -80,18 +79,20 @@
     )(signal, rate, own, other, *base)
 
 
-def image_kernel(
-    place_ref,
-    noise_ref,
-    near_ref,
-    near_other_ref,
-    far_ref,
-    factors_ref,
-    leaf_ref,
-    direction_ref,
-    residual_ref,
-    image_ref,
-    stats_ref,
+def spread(levels, factors_ref, here):
+    total = None
+    for k in range(0, 4, 2):
+        pair = jnp.concatenate(levels[k : k + 2], axis=1)
+        basis = jnp.concatenate([factors_ref[k, here, :], factors_ref[k + 1, here, :]], axis=1)
+        part = lax.dot_general(
+            pair, basis, (((1,), (1,)), ((), ())), preferred_element_type=F32
+        )
+        total = part if total is None else total + part
+    return total
+
+
+def near_kernel(
+    place_ref, noise_ref, near_ref, near_other_ref, factors_ref, leaf_ref, direction_ref, out_ref
 ):
     first = place_ref[0] == 0
     levels = []
@@ -100,20 +101,22 @@
         low = jnp.where(first, own, other)
         high = jnp.where(first, other, own)
         levels.append(jnp.concatenate([low, high], axis=0).astype(BF))
-    levels += [far_ref[k] for k in range(4)]
-    pairs = [jnp.concatenate(levels[k : k + 2], axis=1) for k in range(0, 8, 2)]
-    points = direction_ref.shape[1]
+    for start in range(0, direction_ref.shape[1], 256):
+        here = slice(start, start + 256)
+        base = noise_ref[...] * direction_ref[:, here] + leaf_ref[:, here]
+        out_ref[:, here] = base + spread(levels, factors_ref, here)
+
+
+def image_kernel(
+    far_ref, factors_ref, base_ref, direction_ref, residual_ref, image_ref, stats_ref
+):
+    levels = [far_ref[k] for k in range(4)]
     tile = 256
     sums = [jnp.zeros((64, 128), F32) for _ in range(4)]
-    for start in range(0, points, tile):
+    for start in range(0, direction_ref.shape[1], tile):
         here = slice(start, start + tile)
         direction, residual = direction_ref[:, here], residual_ref[:, here]
-        image = noise_ref[0] * direction + leaf_ref[:, here]
-        for k in range(0, 8, 2):
-            basis = jnp.concatenate([factors_ref[k, here, :], factors_ref[k + 1, here, :]], axis=1)
-            image += lax.dot_general(
-                pairs[k // 2], basis, (((1,), (1,)), ((), ())), preferred_element_type=F32
-            )
+        image = base_ref[:, here] + spread(levels, factors_ref.at[4:8], here)
         image_ref[:, here] = image
         products = [residual * residual, direction * image, residual * image, image * image]
         for n, product in enumerate(products):
@@ -173,8 +176,8 @@
     )(*operands)
 
 
-def meets(mine, order):
-    apart = jnp.bitwise_xor(jnp.array(order, dtype=jnp.int32)[:, None], mine)
+def meets(mine):
+    apart = jnp.bitwise_xor(jnp.arange(16, dtype=jnp.int32)[:, None], mine)
     low = jnp.left_shift(1, jnp.arange(4, dtype=jnp.int32))[None, :]
     return (apart >= low) & (apart < 2 * low)
 
@@ -188,8 +191,8 @@
     projection = jnp.einsum(
         "cp,lpr->lcr", direction.astype(BF), factors, preferred_element_type=F32
     ).astype(BF)
-    near_meets = meets(lax.axis_index(CHIP), CHIPS).reshape(16, 1, 4, 1, 1)
-    far_meets = meets(lax.axis_index("z"), PLANES).reshape(16, 4, 1, 1)
+    near_meets = meets(lax.axis_index(CHIP) ^ 15).reshape(16, 1, 4, 1, 1)
+    far_meets = meets(lax.axis_index("z") ^ 8).reshape(16, 4, 1, 1)
     near = projection[:4].reshape(4, 2, 32, 128).transpose(1, 0, 2, 3)[None]
     near = jnp.sum(jnp.where(near_meets, near, 0.0).astype(F32), axis=2).astype(BF)
     far = projection[4:].reshape(4, 2, 32, 128).transpose(2, 0, 1, 3)
@@ -198,10 +201,10 @@
 
     own = jnp.concatenate([features] + parts_of(lax.optimization_barrier(direction), 2), axis=0)
     other = lax.ppermute(own, "core", SWAP)
+    signal, noise = signal_var.reshape(1, 1), noise_var.reshape(1, 1)
     rate = (LOG2E / (lengthscale * lengthscale))[:, None]
-    leaf = leaf_term(signal_var, rate, own, own)
+    leaf = leaf_term(signal, rate, own, own)
     got, leaf = lax.optimization_barrier((got, leaf))
-    leaf = leaf_term(signal_var, rate, own, other, leaf)
 
     plane_sum = jnp.sum(got[:, 32:].astype(F32), axis=0).reshape(1, 4, 2, 128)
     far = jnp.sum(jnp.where(far_meets, plane_sum, 0.0), axis=1).astype(BF)
@@ -211,6 +214,12 @@
     near = jnp.sum(jnp.where(near_meets.reshape(16, 4, 1, 1), near, 0.0), axis=0)
     near = (gains[:4, None, :] * near).astype(BF)
     near_other = lax.ppermute(near, "core", SWAP)
+    leaf = leaf_term(signal, rate, own, other, leaf)
+    base = call(
+        near_kernel, [((64, 1024), F32)], [SMEM] + [VMEM] * 6,
+        place, noise, near, near_other, factors, leaf, direction, flops=2**26,
+    )
+    far, base = lax.optimization_barrier((far, base))
 
     far = jnp.sum(jnp.where(far_meets, far.astype(F32)[:, None], 0.0), axis=0)
     far = (gains[4:, None, :] * far).astype(BF).reshape(1, 8, 128)
@@ -219,8 +228,8 @@
 
     image, stats = call(
         image_kernel, [((64, 1024), F32), ((16, 1, 256), F32)],
-        [SMEM, SMEM] + [VMEM] * 7,
-        place, noise_var, near, near_other, far, factors, leaf, direction, residual, flops=2**27,
+        [VMEM] * 5,
+        far, factors, base, direction, residual, flops=2**26,
     )
     stats = lax.all_to_all(stats, CHIP, 0, 0, tiled=True, axis_index_groups=[SQUARE]).sum(0)
     stats = jnp.broadcast_to(stats[None], (32, 1, 256))

time: 83.5 us -> 83.5 us (level)
  blocking collectives: 25.5 us -> 36.1 us
  starting transfers between devices: 40.2 us -> 33 us
  local copies, waits for them, and re-layouts: 2.69 us -> 0.96 us
  Pallas kernels: 7.23 us -> 6.39 us
    all_to_all x0 -> x1, blocking collectives: none -> 10.8 us  [local(): lax.all_to_all(jnp.broadcast_to(far, (32, 8, 128)), LEAF, 0, 0, tiled=Tru...]
    all_to_all x1 -> x0, starting transfers between devices: 7.22 us -> none  [local(): lax.all_to_all(jnp.broadcast_to(far, (32, 8, 128)), LEAF, 0, 0, tiled=Tru...]
    unnamed x18 -> x14, local copies, waits for them, and re-layouts: 1.14 us -> 0.03 us
    pallas_call x2, Pallas kernels: 5.05 us -> 4.07 us  [leaf_term(): pl.pallas_call(leaf_kernel, out_shape=jax.ShapeDtypeStruct((64, own.shape...]
    pallas_call x2 -> x3, Pallas kernels: 2.19 us -> 2.32 us  [call(): pl.pallas_call(kernel, out_shape=shapes[0] if single else shapes, in_spec...]
  transfers between devices with their start and end apart: 5 -> 4, of which waited for: 1 -> 1; matrix products, arithmetic and copies ran while one was open for 2% -> 1% of each run, Pallas kernels for 6% -> 5%
where the time goes in v4:
time: 83.5 us; the launch traced here: 83.1 us
  blocking collectives  36.1 us (43%)
  starting transfers between devices  33 us (40%)
  Pallas kernels  6.39 us (8%)
  between operations  2.22 us (3%)
  matrix products  2.2 us (3%)
  other arithmetic  1.6 us (2%)
  local copies, waits for them, and re-layouts  0.96 us (1%)
    all_to_all x1, blocking collectives, local(): lax.all_to_all(stats, ('core', 'z'), 0, 0, tiled=True, axis_index_groups=...  16.2 us
    all_to_all x1, starting transfers between devices, local(): far = lax.all_to_all(far, 'z', 0, 0, tiled=True, axis_index_groups=[PLANES])  14.9 us
    all_to_all x1, starting transfers between devices, local(): lax.all_to_all(sent, LEAF, 0, 0, tiled=True, axis_index_groups=[LEAVES])  13.4 us
    all_to_all x1, blocking collectives, local(): lax.all_to_all(jnp.broadcast_to(far, (32, 8, 128)), LEAF, 0, 0, tiled=Tru...  10.8 us
    all_to_all x1, blocking collectives, local(): lax.all_to_all(stats, CHIP, 0, 0, tiled=True, axis_index_groups=[SQUARE])  9.12 us
    pallas_call x2, Pallas kernels, leaf_term(): pl.pallas_call(leaf_kernel, out_shape=jax.ShapeDtypeStruct((64, own.shape...  4.07 us
    ppermute x1, starting transfers between devices, local(): near_other = lax.ppermute(near, 'core', SWAP)  2.4 us
    pallas_call x3, Pallas kernels, call(): pl.pallas_call(kernel, out_shape=shapes[0] if single else shapes, in_spec...  2.32 us
  transfers between devices with their start and end apart: 4, of which 1 were waited for; matrix products, arithmetic and copies ran while one was open for 1% of the time, Pallas kernels for 5%

profile of v4, /device:TPU:1, one launch (start us, length us, event | category | flops | bytes accessed | tf_op | source)
XLA Modules:
  0.0 83.1 jit_solution(16115326646003673266)
XLA Ops:
  0.7 0.1 compare_and_fusion.1
  0.7 0.1 copy.28
  0.8 2.2 %fusion = bf16[8,64,128]{2,1,0:T(8,128)(2,1)S(1)} fusion(bf16[8,1024,128]{2,1,0:T(8,128)(2,1)} %factors_ref.3, f32[64,1024]{1,0:T(8,128)} %direction_ref.5), kind=kOutput, calls=%fused_computation.1 | convolution fusion | flops 134348800 | bytes 2490368 | tf_op jit(solution)/shard_map/cp,lpr->lcr/dot_general | solution.py:191
  3.1 0.0 copy-start.6
  3.1 0.1 copy.30
  3.1 0.3 select_reduce_fusion.1
  3.4 0.7 pad_maximum_fusion.1
  4.2 13.4 %all-to-all-start = ((bf16[32,40,128]{2,1,0:T(8,128)(2,1)}), bf16[32,40,128]{2,1,0:T(8,128)(2,1)S(1)}, u32[]{:S(2)}, u32[]{:S(2)}) async-start(bf16[32,40,128]{2,1,0:T(8,128)(2,1)} %pad_maximum_fusion.1), calls=%async_computation | async-start | bytes 655360 | tf_op jit(solution)/shard_map/all_to_all | solution.py:200
  17.6 0.0 copy-done.1
  17.6 2.3 %collective-permute-start.1 = (bf16[192,1024]{1,0:T(8,128)(2,1)S(1)}, bf16[192,1024]{1,0:T(8,128)(2,1)S(1)}, u32[]{:S(2)}, u32[]{:S(2)}) collective-permute-start(bf16[192,1024]{1,0:T(8,128)(2,1)S(1)} %pad_maximum_fusion.own_ref.other_ref), channel_id=1, source_target_pairs={{0,16},{16,0},{1,17},{17,1},{2,18},{18,2},{3,19},{19,3},{4,20},{20... | collective-permute-start | bytes 1179656 | tf_op jit(solution)/shard_map/ppermute | solution.py:203
  21.2 0.0 copy-done.6
  21.2 0.1 copy.31.rate_ref
  21.3 2.0 %shard_map.112.refs_0_ = f32[64,1024]{1,0:T(8,128)S(1)} custom-call(f32[1,1]{1,0:T(1,128)} %bitcast.28.signal_ref, f32[64,1]{1,0:T(8,128)S(1)} %copy.31.rate_ref, bf16[192,1024]{1,0:T(8,128)(2,1)S(1)} %pad_maximum_fusion.own_ref.other_ref, bf16[192,1024]{1,0:T(8,128)(2,1)S(1)} %pad_maximum_fusion.own_ref.other_ref), custom_call_target="tpu_custom_call" | custom-call | flops 1610612736 | bytes 1048576 | tf_op jit(solution)/shard_map/pallas_call | solution.py:70
  23.4 0.6 all-to-all-done
  24.1 0.1 select_reduce_fusion.3
  24.2 0.6 copy.32
  24.8 14.9 %all-to-all-start.1 = ((bf16[16,2,128]{2,1,0:T(2,128)(2,1)}), bf16[16,2,128]{2,1,0:T(2,128)(2,1)S(1)}, u32[]{:S(2)}, u32[]{:S(2)}) async-start(bf16[16,2,128]{2,1,0:T(2,128)(2,1)} %copy.32), calls=%async_computation.1 | async-start | bytes 16384 | tf_op jit(solution)/shard_map/all_to_all | solution.py:211
  39.7 0.1 select_reduce_fusion
  39.9 2.4 %collective-permute-start = (bf16[4,32,128]{2,1,0:T(8,128)(2,1)S(1)}, bf16[4,32,128]{2,1,0:T(8,128)(2,1)S(1)}, u32[]{:S(2)}, u32[]{:S(2)}) collective-permute-start(bf16[4,32,128]{2,1,0:T(8,128)(2,1)S(1)} %multiply_convert_fusion.near_ref), channel_id=1, source_target_pairs={{0,16},{16,0},{1,17},{17,1},{2,18},{18,2},{3,19},{19,3},{4,20},{20... | collective-permute-start | bytes 98312 | tf_op jit(solution)/shard_map/ppermute | solution.py:216
  42.3 0.0 collective-permute-done.1.other_ref
  42.3 0.0 copy-start
  42.3 2.0 %shard_map.113.leaf_ref = f32[64,1024]{1,0:T(8,128)S(1)} custom-call(f32[1,1]{1,0:T(1,128)} %bitcast.29.signal_ref, f32[64,1]{1,0:T(8,128)S(1)} %copy.31.rate_ref, bf16[192,1024]{1,0:T(8,128)(2,1)S(1)} %pad_maximum_fusion.own_ref.other_ref, bf16[192,1024]{1,0:T(8,128)(2,1)S(1)} %collective-permute-done.1.other_ref, f32[64,1024]{1,0:T(8,128)S(1)} %shard_map.112.refs_0_), custom_call_target="tpu_custom_call" | custom-call | flops 1610612736 | bytes 1048576 | tf_op jit(solution)/shard_map/pallas_call | solution.py:70
  44.3 0.0 copy-start.2
  44.4 0.0 collective-permute-done.near_other_ref
  44.4 0.4 shard_map.114.base_ref
  44.8 0.0 all-to-all-done.1
  44.9 0.1 select_reduce_fusion.2
  45.0 10.8 %all_to_all.25 = bf16[32,8,128]{2,1,0:T(8,128)(2,1)S(1)} all-to-all(bf16[32,8,128]{2,1,0:T(8,128)(2,1)S(1)} %broadcast_in_dim.112), channel_id=1, replica_groups={{480,496,448,464,416,432,384,400,352,368,320,336,288,304,256,272,224,24..., dimensions={0} | all-to-all | bytes 131072 | tf_op jit(solution)/shard_map/all_to_all | solution.py:226
  55.9 0.6 shard_map.115
  56.4 9.1 %all_to_all.26 = f32[16,1,256]{2,1,0:T(1,128)S(1)} all-to-all(f32[16,1,256]{2,1,0:T(1,128)S(1)} %get-tuple-element.13), channel_id=1, replica_groups={{480,448,416,384,352,320,288,256,224,192,160,128,96,64,32,0},{481,449,4..., dimensions={0} | all-to-all | bytes 32768 | tf_op jit(solution)/shard_map/all_to_all | solution.py:234
  65.6 16.2 %all_to_all.27.stats_ref = f32[32,1,256]{2,1,0:T(1,128)S(1)} all-to-all(f32[32,1,256]{2,1,0:T(1,128)S(1)} %broadcast_in_dim.113), channel_id=1, replica_groups={{24,25,26,27,28,29,30,31,16,17,18,19,20,21,22,23,8,9,10,11,12,13,14,15,..., dimensions={0} | all-to-all | bytes 65536 | tf_op jit(solution)/shard_map/all_to_all | solution.py:236
  81.7 1.3 %shard_map.116 = (f32[64,1024]{1,0:T(8,128)}, f32[64,1024]{1,0:T(8,128)}, f32[64,1024]{1,0:T(8,128)}) custom-call(f32[32,1,256]{2,1,0:T(1,128)S(1)} %all_to_all.27.stats_ref, f32[64,1024]{1,0:T(8,128)S(1)} %copy-done.3, f32[64,1024]{1,0:T(8,128)S(1)} %copy-done.2, f32[64,1024]{1,0:T(8,128)S(1)} %copy-done.1, f32[64,1024]{1,0:T(8,128)S(1)} %get-tuple-element.14.image_ref), custom_call_target="tpu_custom_call" | custom-call | bytes 1867776 | tf_op jit(solution)/shard_map/pallas_call | solution.py:168
  (25 shorter events, 0.3 us)
Async XLA Ops:
  0.8 16.7 %copy-start.1 = (f32[64,1024]{1,0:T(8,128)S(1)}, f32[64,1024]{1,0:T(8,128)}, u32[]{:S(2)}) copy-start(f32[64,1024]{1,0:T(8,128)} %direction_ref.5) | copy-start | bytes 786436
  0.8 16.8 %copy-start.4 = (bf16[64,1024]{1,0:T(8,128)(2,1)S(1)}, bf16[64,1024]{1,0:T(8,128)(2,1)}, u32[]{:S(2)}) copy-start(bf16[64,1024]{1,0:T(8,128)(2,1)} %param.9) | copy-start | bytes 393220
  3.1 18.2 %copy-start.6 = (f32[64]{0:T(128)S(1)}, f32[64]{0:T(128)}, u32[]{:S(2)}) copy-start(f32[64]{0:T(128)} %param.10) | copy-start | bytes 772
  4.2 19.8 %all-to-all-start = ((bf16[32,40,128]{2,1,0:T(8,128)(2,1)}), bf16[32,40,128]{2,1,0:T(8,128)(2,1)S(1)}, u32[]{:S(2)}, u32[]{:S(2)}) async-start(bf16[32,40,128]{2,1,0:T(8,128)(2,1)} %pad_maximum_fusion.1), calls=%async_computation | async-start | bytes 655360 | tf_op jit(solution)/shard_map/all_to_all | solution.py:200
  17.6 24.6 %collective-permute-start.1 = (bf16[192,1024]{1,0:T(8,128)(2,1)S(1)}, bf16[192,1024]{1,0:T(8,128)(2,1)S(1)}, u32[]{:S(2)}, u32[]{:S(2)}) collective-permute-start(bf16[192,1024]{1,0:T(8,128)(2,1)S(1)} %pad_maximum_fusion.own_ref.other_ref), channel_id=1, source_target_pairs={{0,16},{16,0},{1,17},{17,1},{2,18},{18,2},{3,19},{19,3},{4,20},{20... | collective-permute-start | bytes 1179656 | tf_op jit(solution)/shard_map/ppermute | solution.py:203
  21.3 2.0 %copy-start.5 = (f32[8,128]{1,0:T(8,128)S(1)}, f32[8,128]{1,0:T(8,128)}, u32[]{:S(2)}) copy-start(f32[8,128]{1,0:T(8,128)} %param.14) | copy-start | bytes 12292
  24.8 20.1 %all-to-all-start.1 = ((bf16[16,2,128]{2,1,0:T(2,128)(2,1)}), bf16[16,2,128]{2,1,0:T(2,128)(2,1)S(1)}, u32[]{:S(2)}, u32[]{:S(2)}) async-start(bf16[16,2,128]{2,1,0:T(2,128)(2,1)} %copy.32), calls=%async_computation.1 | async-start | bytes 16384 | tf_op jit(solution)/shard_map/all_to_all | solution.py:211
  39.9 4.5 %collective-permute-start = (bf16[4,32,128]{2,1,0:T(8,128)(2,1)S(1)}, bf16[4,32,128]{2,1,0:T(8,128)(2,1)S(1)}, u32[]{:S(2)}, u32[]{:S(2)}) collective-permute-start(bf16[4,32,128]{2,1,0:T(8,128)(2,1)S(1)} %multiply_convert_fusion.near_ref), channel_id=1, source_target_pairs={{0,16},{16,0},{1,17},{17,1},{2,18},{18,2},{3,19},{19,3},{4,20},{20... | collective-permute-start | bytes 98312 | tf_op jit(solution)/shard_map/ppermute | solution.py:216
  42.3 2.1 %copy-start = (bf16[8,1024,128]{2,1,0:T(8,128)(2,1)S(1)}, bf16[8,1024,128]{2,1,0:T(8,128)(2,1)}, u32[]{:S(2)}) copy-start(bf16[8,1024,128]{2,1,0:T(8,128)(2,1)} %factors_ref.3) | copy-start | bytes 6291460
  44.3 11.5 %copy-start.2 = (f32[64,1024]{1,0:T(8,128)S(1)}, f32[64,1024]{1,0:T(8,128)}, u32[]{:S(2)}) copy-start(f32[64,1024]{1,0:T(8,128)} %residual_ref.3) | copy-start | bytes 786436
  44.8 36.9 %copy-start.3 = (f32[64,1024]{1,0:T(8,128)S(1)}, f32[64,1024]{1,0:T(8,128)}, u32[]{:S(2)}) copy-start(f32[64,1024]{1,0:T(8,128)} %solution_ref.1) | copy-start | bytes 786436

commit v5 on v3

--- a/solution.py
+++ b/solution.py
@@ -14,11 +14,10 @@
 SMEM = pl.BlockSpec(memory_space=pltpu.SMEM)
 HBM = pl.BlockSpec(memory_space=pltpu.HBM)
 SWAP = [(0, 1), (1, 0)]
-PLANES = [8, 0, 15, 1, 14, 2, 13, 3, 12, 4, 11, 5, 10, 6, 9, 7]
-COLUMN = [24, 16, 31, 17, 30, 18, 29, 19, 28, 20, 27, 21, 26, 22, 25, 23, 8, 0, 15, 1, 14, 2, 13, 3, 12, 4, 11, 5, 10, 6, 9, 7]
-CHIPS = [15, 14, 13, 12, 11, 10, 9, 8, 7, 6, 5, 4, 3, 2, 1, 0]
-LEAVES = [30, 31, 28, 29, 26, 27, 24, 25, 22, 23, 20, 21, 18, 19, 16, 17, 14, 15, 12, 13, 10, 11, 8, 9, 6, 7, 4, 5, 2, 3, 0, 1]
-SQUARE = [15, 14, 13, 12, 11, 10, 9, 8, 7, 6, 5, 4, 3, 2, 1, 0]
+PLANES = [z ^ 8 for z in range(16)]
+COLUMN = [16 * core + z for core in (1, 0) for z in PLANES]
+LEAVES = [leaf ^ 30 for leaf in range(32)]
+SQUARE = [chip ^ 15 for chip in range(16)]
 BF = jnp.bfloat16
 F32 = jnp.float32
 
@@ -61,7 +60,7 @@
         high, low = parts_of(jnp.exp2(power), 2)
         both = lax.dot_general(high, value, dims, preferred_element_type=F32).T
         rest = lax.dot_general(low, value[0:64], dims, preferred_element_type=F32).T
-        result = signal_ref[0] * (both[0:64] + both[64:128] + rest)
+        result = signal_ref[...] * (both[0:64] + both[64:128] + rest)
         if len(refs) > 1:
             result += refs[0][:, here]
         out_ref[:, here] = result
@@ -71,7 +70,7 @@
     return pl.pallas_call(
         leaf_kernel,
         out_shape=jax.ShapeDtypeStruct((64, own.shape[1]), F32),
-        in_specs=[SMEM] + [VMEM] * (3 + len(base)),
+        in_specs=[VMEM] * (4 + len(base)),
         out_specs=VMEM,
         compiler_params=pltpu.CompilerParams(vmem_limit_bytes=40 * 2**20),
         cost_estimate=pl.CostEstimate(
@@ -108,7 +107,7 @@
     for start in range(0, points, tile):
         here = slice(start, start + tile)
         direction, residual = direction_ref[:, here], residual_ref[:, here]
-        image = noise_ref[0] * direction + leaf_ref[:, here]
+        image = noise_ref[...] * direction + leaf_ref[:, here]
         for k in range(0, 8, 2):
             basis = jnp.concatenate([factors_ref[k, here, :], factors_ref[k + 1, here, :]], axis=1)
             image += lax.dot_general(
@@ -173,8 +172,8 @@
     )(*operands)
 
 
-def meets(mine, order):
-    apart = jnp.bitwise_xor(jnp.array(order, dtype=jnp.int32)[:, None], mine)
+def meets(mine):
+    apart = jnp.bitwise_xor(jnp.arange(16, dtype=jnp.int32)[:, None], mine)
     low = jnp.left_shift(1, jnp.arange(4, dtype=jnp.int32))[None, :]
     return (apart >= low) & (apart < 2 * low)
 
@@ -188,8 +187,8 @@
     projection = jnp.einsum(
         "cp,lpr->lcr", direction.astype(BF), factors, preferred_element_type=F32
     ).astype(BF)
-    near_meets = meets(lax.axis_index(CHIP), CHIPS).reshape(16, 1, 4, 1, 1)
-    far_meets = meets(lax.axis_index("z"), PLANES).reshape(16, 4, 1, 1)
+    near_meets = meets(lax.axis_index(CHIP) ^ 15).reshape(16, 1, 4, 1, 1)
+    far_meets = meets(lax.axis_index("z") ^ 8).reshape(16, 4, 1, 1)
     near = projection[:4].reshape(4, 2, 32, 128).transpose(1, 0, 2, 3)[None]
     near = jnp.sum(jnp.where(near_meets, near, 0.0).astype(F32), axis=2).astype(BF)
     far = projection[4:].reshape(4, 2, 32, 128).transpose(2, 0, 1, 3)
@@ -198,10 +197,11 @@
 
     own = jnp.concatenate([features] + parts_of(lax.optimization_barrier(direction), 2), axis=0)
     other = lax.ppermute(own, "core", SWAP)
+    signal, noise = signal_var.reshape(1, 1), noise_var.reshape(1, 1)
     rate = (LOG2E / (lengthscale * lengthscale))[:, None]
-    leaf = leaf_term(signal_var, rate, own, own)
+    leaf = leaf_term(signal, rate, own, own)
     got, leaf = lax.optimization_barrier((got, leaf))
-    leaf = leaf_term(signal_var, rate, own, other, leaf)
+    leaf = leaf_term(signal, rate, own, other, leaf)
 
     plane_sum = jnp.sum(got[:, 32:].astype(F32), axis=0).reshape(1, 4, 2, 128)
     far = jnp.sum(jnp.where(far_meets, plane_sum, 0.0), axis=1).astype(BF)
@@ -219,8 +219,8 @@
 
     image, stats = call(
         image_kernel, [((64, 1024), F32), ((16, 1, 256), F32)],
-        [SMEM, SMEM] + [VMEM] * 7,
-        place, noise_var, near, near_other, far, factors, leaf, direction, residual, flops=2**27,
+        [SMEM] + [VMEM] * 8,
+        place, noise, near, near_other, far, factors, leaf, direction, residual, flops=2**27,
     )
     stats = lax.all_to_all(stats, CHIP, 0, 0, tiled=True, axis_index_groups=[SQUARE]).sum(0)
     stats = jnp.broadcast_to(stats[None], (32, 1, 256))

time: 83.5 us -> 83.6 us (level)
  local copies, waits for them, and re-layouts: 2.69 us -> 4.27 us
  Pallas kernels: 7.23 us -> 6.27 us
    unnamed x18 -> x22, local copies, waits for them, and re-layouts: 1.14 us -> 2.72 us
    pallas_call x2, Pallas kernels: 5.05 us -> 4.07 us  [leaf_term(): pl.pallas_call(leaf_kernel, out_shape=jax.ShapeDtypeStruct((64, own.shape...]
  transfers between devices with their start and end apart: 5 -> 5, of which waited for: 1 -> 1; matrix products, arithmetic and copies ran while one was open for 2% -> 2% of each run, Pallas kernels for 6% -> 5%
where the time goes in v5:
time: 83.6 us; the launch traced here: 83.1 us
  starting transfers between devices  40.2 us (48%)
  blocking collectives  25.7 us (31%)
  Pallas kernels  6.27 us (8%)
  local copies, waits for them, and re-layouts  4.27 us (5%)
  between operations  2.26 us (3%)
  matrix products  2.2 us (3%)
  other arithmetic  1.61 us (2%)
    all_to_all x1, blocking collectives, local(): lax.all_to_all(stats, ('core', 'z'), 0, 0, tiled=True, axis_index_groups=...  16.1 us
    all_to_all x1, starting transfers between devices, local(): far = lax.all_to_all(far, 'z', 0, 0, tiled=True, axis_index_groups=[PLANES])  14.9 us
    all_to_all x1, starting transfers between devices, local(): lax.all_to_all(sent, LEAF, 0, 0, tiled=True, axis_index_groups=[LEAVES])  13.4 us
    all_to_all x1, blocking collectives, local(): lax.all_to_all(stats, CHIP, 0, 0, tiled=True, axis_index_groups=[SQUARE])  9.64 us
    all_to_all x1, starting transfers between devices, local(): lax.all_to_all(jnp.broadcast_to(far, (32, 8, 128)), LEAF, 0, 0, tiled=Tru...  7.2 us
    pallas_call x2, Pallas kernels, leaf_term(): pl.pallas_call(leaf_kernel, out_shape=jax.ShapeDtypeStruct((64, own.shape...  4.07 us
    unnamed x22, local copies, waits for them, and re-layouts  2.72 us
    ppermute x1, starting transfers between devices, local(): near_other = lax.ppermute(near, 'core', SWAP)  2.4 us
  transfers between devices with their start and end apart: 5, of which 1 were waited for; matrix products, arithmetic and copies ran while one was open for 2% of the time, Pallas kernels for 5%

profile of v5, /device:TPU:1, one launch (start us, length us, event | category | flops | bytes accessed | tf_op | source)
XLA Modules:
  0.0 83.1 jit_solution(5477740821723154732)
XLA Ops:
  0.7 0.1 compare_and_fusion
  0.7 0.1 copy.37
  0.8 2.2 %fusion = bf16[8,64,128]{2,1,0:T(8,128)(2,1)S(1)} fusion(bf16[8,1024,128]{2,1,0:T(8,128)(2,1)} %factors_ref.1, f32[64,1024]{1,0:T(8,128)} %direction_ref.3), kind=kOutput, calls=%fused_computation.1 | convolution fusion | flops 134348800 | bytes 2490368 | tf_op jit(solution)/shard_map/cp,lpr->lcr/dot_general | solution.py:187
  3.1 0.0 copy-start.10
  3.1 0.1 copy.40
  3.1 0.3 select_reduce_fusion.1
  3.4 0.8 pad_maximum_fusion.1
  4.2 13.4 %all-to-all-start = ((bf16[32,40,128]{2,1,0:T(8,128)(2,1)}), bf16[32,40,128]{2,1,0:T(8,128)(2,1)S(1)}, u32[]{:S(2)}, u32[]{:S(2)}) async-start(bf16[32,40,128]{2,1,0:T(8,128)(2,1)} %pad_maximum_fusion.1), calls=%async_computation | async-start | bytes 655360 | tf_op jit(solution)/shard_map/all_to_all | solution.py:196
  17.7 2.3 %collective-permute-start.1 = (bf16[192,1024]{1,0:T(8,128)(2,1)S(1)}, bf16[192,1024]{1,0:T(8,128)(2,1)S(1)}, u32[]{:S(2)}, u32[]{:S(2)}) collective-permute-start(bf16[192,1024]{1,0:T(8,128)(2,1)S(1)} %pad_maximum_fusion.own_ref.other_ref), channel_id=1, source_target_pairs={{0,16},{16,0},{1,17},{17,1},{2,18},{18,2},{3,19},{19,3},{4,20},{20... | collective-permute-start | bytes 1179656 | tf_op jit(solution)/shard_map/ppermute | solution.py:199
  20.0 0.1 copy.41.rate_ref
  21.4 0.0 copy-start.9
  21.4 2.0 %shard_map.112.refs_0_ = f32[64,1024]{1,0:T(8,128)S(1)} custom-call(f32[1,1]{1,0:T(1,128)} %bitcast.28.signal_ref, f32[64,1]{1,0:T(8,128)S(1)} %copy.41.rate_ref, bf16[192,1024]{1,0:T(8,128)(2,1)S(1)} %pad_maximum_fusion.own_ref.other_ref, bf16[192,1024]{1,0:T(8,128)(2,1)S(1)} %pad_maximum_fusion.own_ref.other_ref), custom_call_target="tpu_custom_call" | custom-call | flops 1610612736 | bytes 1048576 | tf_op jit(solution)/shard_map/pallas_call | solution.py:70
  23.4 0.0 copy-start.6
  23.5 0.6 all-to-all-done
  24.1 0.1 select_reduce_fusion.3
  24.2 0.6 copy.42
  24.8 14.9 %all-to-all-start.1 = ((bf16[16,2,128]{2,1,0:T(2,128)(2,1)}), bf16[16,2,128]{2,1,0:T(2,128)(2,1)S(1)}, u32[]{:S(2)}, u32[]{:S(2)}) async-start(bf16[16,2,128]{2,1,0:T(2,128)(2,1)} %copy.42), calls=%async_computation.1 | async-start | bytes 16384 | tf_op jit(solution)/shard_map/all_to_all | solution.py:208
  39.7 0.1 select_reduce_fusion
  39.9 2.4 %collective-permute-start = (bf16[4,32,128]{2,1,0:T(8,128)(2,1)S(1)}, bf16[4,32,128]{2,1,0:T(8,128)(2,1)S(1)}, u32[]{:S(2)}, u32[]{:S(2)}) collective-permute-start(bf16[4,32,128]{2,1,0:T(8,128)(2,1)S(1)} %multiply_convert_fusion.near_ref), channel_id=1, source_target_pairs={{0,16},{16,0},{1,17},{17,1},{2,18},{18,2},{3,19},{19,3},{4,20},{20... | collective-permute-start | bytes 98312 | tf_op jit(solution)/shard_map/ppermute | solution.py:213
  42.3 0.0 all-to-all-done.1
  42.3 0.1 select_reduce_fusion.2
  42.4 0.6 broadcast_in_dim.112
  43.1 7.2 %all-to-all-start.2 = ((bf16[32,8,128]{2,1,0:T(8,128)(2,1)}), bf16[32,8,128]{2,1,0:T(8,128)(2,1)S(1)}, u32[]{:S(2)}, u32[]{:S(2)}) async-start(bf16[32,8,128]{2,1,0:T(8,128)(2,1)} %broadcast_in_dim.112), calls=%async_computation.2 | async-start | bytes 131072 | tf_op jit(solution)/shard_map/all_to_all | solution.py:217
  50.3 0.7 copy-done.4
  51.0 1.0 %copy-done.5 = bf16[192,1024]{1,0:T(8,128)(2,1)S(1)} copy-done((bf16[192,1024]{1,0:T(8,128)(2,1)S(1)}, bf16[192,1024]{1,0:T(8,128)(2,1)}, u32[]{:S(2)}) %copy-start.5) | copy-done | bytes 393240
  52.0 0.9 %copy-done.7 = f32[64,1024]{1,0:T(8,128)S(1)} copy-done((f32[64,1024]{1,0:T(8,128)S(1)}, f32[64,1024]{1,0:T(8,128)}, u32[]{:S(2)}) %copy-start.7) | copy-done | bytes 262168
  53.0 2.0 %shard_map.113.leaf_ref = f32[64,1024]{1,0:T(8,128)S(1)} custom-call(f32[1,1]{1,0:T(1,128)} %bitcast.29.signal_ref, f32[64,1]{1,0:T(8,128)S(1)} %copy.41.rate_ref, bf16[192,1024]{1,0:T(8,128)(2,1)S(1)} %pad_maximum_fusion.own_ref.other_ref, bf16[192,1024]{1,0:T(8,128)(2,1)S(1)} %copy-done.5, f32[64,1024]{1,0:T(8,128)S(1)} %copy-done.7), custom_call_target="tpu_custom_call" | custom-call | flops 1610612736 | bytes 1048576 | tf_op jit(solution)/shard_map/pallas_call | solution.py:70
  55.0 0.0 copy-start.3
  55.1 0.9 %shard_map.114 = (f32[64,1024]{1,0:T(8,128)S(1)}, f32[16,1,256]{2,1,0:T(1,128)S(1)}) custom-call(s32[1]{0:T(128)} %bitcast.place_ref, f32[1,1]{1,0:T(1,128)} %bitcast.30.noise_ref, bf16[4,32,128]{2,1,0:T(8,128)(2,1)S(1)} %multiply_convert_fusion.near_ref, bf16[4,32,128]{2,1,0:T(8,128)(2,1)S(1)} %collective-permute-done.near_other_ref, ...), custom_call_target="tpu_custom_call" | custom-call | flops 134217728 | bytes 3293192 | tf_op jit(solution)/shard_map/pallas_call | solution.py:164
  56.0 9.6 %all_to_all.25 = f32[16,1,256]{2,1,0:T(1,128)S(1)} all-to-all(f32[16,1,256]{2,1,0:T(1,128)S(1)} %get-tuple-element.9), channel_id=1, replica_groups={{480,448,416,384,352,320,288,256,224,192,160,128,96,64,32,0},{481,449,4..., dimensions={0} | all-to-all | bytes 32768 | tf_op jit(solution)/shard_map/all_to_all | solution.py:225
  65.7 16.1 %all_to_all.26.stats_ref = f32[32,1,256]{2,1,0:T(1,128)S(1)} all-to-all(f32[32,1,256]{2,1,0:T(1,128)S(1)} %broadcast_in_dim.113), channel_id=1, replica_groups={{24,25,26,27,28,29,30,31,16,17,18,19,20,21,22,23,8,9,10,11,12,13,14,15,..., dimensions={0} | all-to-all | bytes 65536 | tf_op jit(solution)/shard_map/all_to_all | solution.py:227
  81.7 1.3 %shard_map.115 = (f32[64,1024]{1,0:T(8,128)}, f32[64,1024]{1,0:T(8,128)}, f32[64,1024]{1,0:T(8,128)}) custom-call(f32[32,1,256]{2,1,0:T(1,128)S(1)} %all_to_all.26.stats_ref, f32[64,1024]{1,0:T(8,128)S(1)} %copy-done.3, f32[64,1024]{1,0:T(8,128)S(1)} %copy-done.2, f32[64,1024]{1,0:T(8,128)S(1)} %copy-done.1, f32[64,1024]{1,0:T(8,128)S(1)} %get-tuple-element.10.image_ref), custom_call_target="tpu_custom_call" | custom-call | bytes 1867776 | tf_op jit(solution)/shard_map/pallas_call | solution.py:164
  (33 shorter events, 0.3 us)
Async XLA Ops:
  0.8 16.7 %copy-start.1 = (f32[64,1024]{1,0:T(8,128)S(1)}, f32[64,1024]{1,0:T(8,128)}, u32[]{:S(2)}) copy-start(f32[64,1024]{1,0:T(8,128)} %direction_ref.3) | copy-start | bytes 786436
  0.8 16.8 %copy-start.8 = (bf16[64,1024]{1,0:T(8,128)(2,1)S(1)}, bf16[64,1024]{1,0:T(8,128)(2,1)}, u32[]{:S(2)}) copy-start(bf16[64,1024]{1,0:T(8,128)(2,1)} %param.9) | copy-start | bytes 393220
  3.1 16.9 %copy-start.10 = (f32[64]{0:T(128)S(1)}, f32[64]{0:T(128)}, u32[]{:S(2)}) copy-start(f32[64]{0:T(128)} %param.10) | copy-start | bytes 772
  4.2 19.8 %all-to-all-start = ((bf16[32,40,128]{2,1,0:T(8,128)(2,1)}), bf16[32,40,128]{2,1,0:T(8,128)(2,1)S(1)}, u32[]{:S(2)}, u32[]{:S(2)}) async-start(bf16[32,40,128]{2,1,0:T(8,128)(2,1)} %pad_maximum_fusion.1), calls=%async_computation | async-start | bytes 655360 | tf_op jit(solution)/shard_map/all_to_all | solution.py:196
  17.7 32.6 %collective-permute-start.1 = (bf16[192,1024]{1,0:T(8,128)(2,1)S(1)}, bf16[192,1024]{1,0:T(8,128)(2,1)S(1)}, u32[]{:S(2)}, u32[]{:S(2)}) collective-permute-start(bf16[192,1024]{1,0:T(8,128)(2,1)S(1)} %pad_maximum_fusion.own_ref.other_ref), channel_id=1, source_target_pairs={{0,16},{16,0},{1,17},{17,1},{2,18},{18,2},{3,19},{19,3},{4,20},{20... | collective-permute-start | bytes 1179656 | tf_op jit(solution)/shard_map/ppermute | solution.py:199
  21.4 2.1 %copy-start.9 = (f32[8,128]{1,0:T(8,128)S(1)}, f32[8,128]{1,0:T(8,128)}, u32[]{:S(2)}) copy-start(f32[8,128]{1,0:T(8,128)} %param.14) | copy-start | bytes 12292
  23.4 26.9 %copy-start.6 = (f32[64,1024]{1,0:T(8,128)}, f32[64,1024]{1,0:T(8,128)S(1)}, u32[]{:S(2)}) copy-start(f32[64,1024]{1,0:T(8,128)S(1)} %shard_map.112.refs_0_) | copy-start | bytes 786436
  24.8 17.5 %all-to-all-start.1 = ((bf16[16,2,128]{2,1,0:T(2,128)(2,1)}), bf16[16,2,128]{2,1,0:T(2,128)(2,1)S(1)}, u32[]{:S(2)}, u32[]{:S(2)}) async-start(bf16[16,2,128]{2,1,0:T(2,128)(2,1)} %copy.42), calls=%async_computation.1 | async-start | bytes 16384 | tf_op jit(solution)/shard_map/all_to_all | solution.py:208
  39.9 15.2 %collective-permute-start = (bf16[4,32,128]{2,1,0:T(8,128)(2,1)S(1)}, bf16[4,32,128]{2,1,0:T(8,128)(2,1)S(1)}, u32[]{:S(2)}, u32[]{:S(2)}) collective-permute-start(bf16[4,32,128]{2,1,0:T(8,128)(2,1)S(1)} %multiply_convert_fusion.near_ref), channel_id=1, source_target_pairs={{0,16},{16,0},{1,17},{17,1},{2,18},{18,2},{3,19},{19,3},{4,20},{20... | collective-permute-start | bytes 98312 | tf_op jit(solution)/shard_map/ppermute | solution.py:213
  43.1 12.0 %all-to-all-start.2 = ((bf16[32,8,128]{2,1,0:T(8,128)(2,1)}), bf16[32,8,128]{2,1,0:T(8,128)(2,1)S(1)}, u32[]{:S(2)}, u32[]{:S(2)}) async-start(bf16[32,8,128]{2,1,0:T(8,128)(2,1)} %broadcast_in_dim.112), calls=%async_computation.2 | async-start | bytes 131072 | tf_op jit(solution)/shard_map/all_to_all | solution.py:217
  50.3 0.7 copy-start.4
  51.0 1.0 %copy-start.5 = (bf16[192,1024]{1,0:T(8,128)(2,1)S(1)}, bf16[192,1024]{1,0:T(8,128)(2,1)}, u32[]{:S(2)}) copy-start(bf16[192,1024]{1,0:T(8,128)(2,1)} %copy-done.4) | copy-start | bytes 1179652
  52.0 0.9 %copy-start.7 = (f32[64,1024]{1,0:T(8,128)S(1)}, f32[64,1024]{1,0:T(8,128)}, u32[]{:S(2)}) copy-start(f32[64,1024]{1,0:T(8,128)} %copy-done.6) | copy-start | bytes 786436
  53.0 2.1 %copy-start = (bf16[8,1024,128]{2,1,0:T(8,128)(2,1)S(1)}, bf16[8,1024,128]{2,1,0:T(8,128)(2,1)}, u32[]{:S(2)}) copy-start(bf16[8,1024,128]{2,1,0:T(8,128)(2,1)} %factors_ref.1) | copy-start | bytes 6291460
  53.0 2.1 %copy-start.2 = (f32[64,1024]{1,0:T(8,128)S(1)}, f32[64,1024]{1,0:T(8,128)}, u32[]{:S(2)}) copy-start(f32[64,1024]{1,0:T(8,128)} %residual_ref.3) | copy-start | bytes 786436
  55.0 26.7 %copy-start.3 = (f32[64,1024]{1,0:T(8,128)S(1)}, f32[64,1024]{1,0:T(8,128)}, u32[]{:S(2)}) copy-start(f32[64,1024]{1,0:T(8,128)} %solution_ref.1) | copy-start | bytes 786436

commit v6 on v3

--- a/solution.py
+++ b/solution.py
@@ -14,7 +14,7 @@
 SMEM = pl.BlockSpec(memory_space=pltpu.SMEM)
 HBM = pl.BlockSpec(memory_space=pltpu.HBM)
 SWAP = [(0, 1), (1, 0)]
-PLANES = [8, 0, 15, 1, 14, 2, 13, 3, 12, 4, 11, 5, 10, 6, 9, 7]
+PLANES = [(8 - slot) % 16 for slot in range(16)]
 COLUMN = [24, 16, 31, 17, 30, 18, 29, 19, 28, 20, 27, 21, 26, 22, 25, 23, 8, 0, 15, 1, 14, 2, 13, 3, 12, 4, 11, 5, 10, 6, 9, 7]
 CHIPS = [15, 14, 13, 12, 11, 10, 9, 8, 7, 6, 5, 4, 3, 2, 1, 0]
 LEAVES = [30, 31, 28, 29, 26, 27, 24, 25, 22, 23, 20, 21, 18, 19, 16, 17, 14, 15, 12, 13, 10, 11, 8, 9, 6, 7, 4, 5, 2, 3, 0, 1]
@@ -173,8 +173,9 @@
     )(*operands)
 
 
-def meets(mine, order):
-    apart = jnp.bitwise_xor(jnp.array(order, dtype=jnp.int32)[:, None], mine)
+def meets(mine, first):
+    slot = jnp.arange(16, dtype=jnp.int32)[:, None]
+    apart = jnp.bitwise_xor(jnp.bitwise_and(first - slot, 15), mine)
     low = jnp.left_shift(1, jnp.arange(4, dtype=jnp.int32))[None, :]
     return (apart >= low) & (apart < 2 * low)
 
@@ -188,8 +189,8 @@
     projection = jnp.einsum(
         "cp,lpr->lcr", direction.astype(BF), factors, preferred_element_type=F32
     ).astype(BF)
-    near_meets = meets(lax.axis_index(CHIP), CHIPS).reshape(16, 1, 4, 1, 1)
-    far_meets = meets(lax.axis_index("z"), PLANES).reshape(16, 4, 1, 1)
+    near_meets = meets(lax.axis_index(CHIP), 15).reshape(16, 1, 4, 1, 1)
+    far_meets = meets(lax.axis_index("z"), 8).reshape(16, 4, 1, 1)
     near = projection[:4].reshape(4, 2, 32, 128).transpose(1, 0, 2, 3)[None]
     near = jnp.sum(jnp.where(near_meets, near, 0.0).astype(F32), axis=2).astype(BF)
     far = projection[4:].reshape(4, 2, 32, 128).transpose(2, 0, 1, 3)

time: 83.5 us -> 82.8 us (level)
  no operation moved by 1% of the time
where the time goes in v6:
time: 82.8 us; the launch traced here: 82.3 us
  starting transfers between devices  40.2 us (49%)
  blocking collectives  25.5 us (31%)
  Pallas kernels  7.23 us (9%)
  local copies, waits for them, and re-layouts  2.69 us (3%)
  between operations  2.26 us (3%)
  matrix products  2.2 us (3%)
  other arithmetic  1.62 us (2%)
    all_to_all x1, blocking collectives, local(): lax.all_to_all(stats, ('core', 'z'), 0, 0, tiled=True, axis_index_groups=...  15.9 us
    all_to_all x1, starting transfers between devices, local(): far = lax.all_to_all(far, 'z', 0, 0, tiled=True, axis_index_groups=[PLANES])  14.9 us
    all_to_all x1, starting transfers between devices, local(): lax.all_to_all(sent, LEAF, 0, 0, tiled=True, axis_index_groups=[LEAVES])  13.4 us
    all_to_all x1, blocking collectives, local(): lax.all_to_all(stats, CHIP, 0, 0, tiled=True, axis_index_groups=[SQUARE])  9.64 us
    all_to_all x1, starting transfers between devices, local(): lax.all_to_all(jnp.broadcast_to(far, (32, 8, 128)), LEAF, 0, 0, tiled=Tru...  7.23 us
    pallas_call x2, Pallas kernels, leaf_term(): pl.pallas_call(leaf_kernel, out_shape=jax.ShapeDtypeStruct((64, own.shape...  5.04 us
    ppermute x1, starting transfers between devices, local(): near_other = lax.ppermute(near, 'core', SWAP)  2.4 us
    ppermute x1, starting transfers between devices, local(): other = lax.ppermute(own, 'core', SWAP)  2.27 us
  transfers between devices with their start and end apart: 5, of which 1 were waited for; matrix products, arithmetic and copies ran while one was open for 2% of the time, Pallas kernels for 6%

profile of v6, /device:TPU:1, one launch (start us, length us, event | category | flops | bytes accessed | tf_op | source)
XLA Modules:
  0.0 82.3 jit_solution(6677863771215296250)
XLA Ops:
  0.7 0.1 compare_and_fusion
  0.7 0.1 copy.37
  0.8 2.2 %fusion = bf16[8,64,128]{2,1,0:T(8,128)(2,1)S(1)} fusion(bf16[8,1024,128]{2,1,0:T(8,128)(2,1)} %factors_ref.1, f32[64,1024]{1,0:T(8,128)} %direction_ref.3), kind=kOutput, calls=%fused_computation.1 | convolution fusion | flops 134348800 | bytes 2490368 | tf_op jit(solution)/shard_map/cp,lpr->lcr/dot_general | solution.py:189
  3.1 0.0 copy-start.8
  3.1 0.1 copy.40
  3.1 0.3 select_reduce_fusion.1
  3.4 0.8 pad_maximum_fusion.1
  4.2 13.4 %all-to-all-start = ((bf16[32,40,128]{2,1,0:T(8,128)(2,1)}), bf16[32,40,128]{2,1,0:T(8,128)(2,1)S(1)}, u32[]{:S(2)}, u32[]{:S(2)}) async-start(bf16[32,40,128]{2,1,0:T(8,128)(2,1)} %pad_maximum_fusion.1), calls=%async_computation | async-start | bytes 655360 | tf_op jit(solution)/shard_map/all_to_all | solution.py:198
  17.7 2.3 %collective-permute-start.1 = (bf16[192,1024]{1,0:T(8,128)(2,1)S(1)}, bf16[192,1024]{1,0:T(8,128)(2,1)}, u32[]{:S(2)}, u32[]{:S(2)}) collective-permute-start(bf16[192,1024]{1,0:T(8,128)(2,1)S(1)} %pad_maximum_fusion.own_ref.other_ref), channel_id=1, source_target_pairs={{0,16},{16,0},{1,17},{17,1},{2,18},{18,2},{3,19},{19,3},{4,20},{20... | collective-permute-start | bytes 1179656 | tf_op jit(solution)/shard_map/ppermute | solution.py:201
  20.0 0.1 copy.41.rate_ref
  21.4 0.0 copy-start.7
  21.4 2.0 %shard_map.112.refs_0_ = f32[64,1024]{1,0:T(8,128)S(1)} custom-call(f32[1]{0:T(128)S(6)} %copy.49.signal_ref, f32[64,1]{1,0:T(8,128)S(1)} %copy.41.rate_ref, bf16[192,1024]{1,0:T(8,128)(2,1)S(1)} %pad_maximum_fusion.own_ref.other_ref, bf16[192,1024]{1,0:T(8,128)(2,1)S(1)} %pad_maximum_fusion.own_ref.other_ref), custom_call_target="tpu_custom_call" | custom-call | flops 1610612736 | bytes 1048576 | tf_op jit(solution)/shard_map/pallas_call | solution.py:71
  23.4 0.0 copy-start.4
  23.4 0.6 all-to-all-done
  24.1 0.1 select_reduce_fusion.3
  24.2 0.6 copy.42
  24.8 14.9 %all-to-all-start.1 = ((bf16[16,2,128]{2,1,0:T(2,128)(2,1)}), bf16[16,2,128]{2,1,0:T(2,128)(2,1)S(1)}, u32[]{:S(2)}, u32[]{:S(2)}) async-start(bf16[16,2,128]{2,1,0:T(2,128)(2,1)} %copy.42), calls=%async_computation.1 | async-start | bytes 16384 | tf_op jit(solution)/shard_map/all_to_all | solution.py:209
  39.7 0.1 select_reduce_fusion
  39.9 2.4 %collective-permute-start = (bf16[4,32,128]{2,1,0:T(8,128)(2,1)S(1)}, bf16[4,32,128]{2,1,0:T(8,128)(2,1)S(1)}, u32[]{:S(2)}, u32[]{:S(2)}) collective-permute-start(bf16[4,32,128]{2,1,0:T(8,128)(2,1)S(1)} %multiply_convert_fusion.near_ref), channel_id=1, source_target_pairs={{0,16},{16,0},{1,17},{17,1},{2,18},{18,2},{3,19},{19,3},{4,20},{20... | collective-permute-start | bytes 98312 | tf_op jit(solution)/shard_map/ppermute | solution.py:214
  42.3 0.1 select_reduce_fusion.2
  42.4 0.6 broadcast_in_dim.112
  43.1 7.2 %all-to-all-start.2 = ((bf16[32,8,128]{2,1,0:T(8,128)(2,1)}), bf16[32,8,128]{2,1,0:T(8,128)(2,1)S(1)}, u32[]{:S(2)}, u32[]{:S(2)}) async-start(bf16[32,8,128]{2,1,0:T(8,128)(2,1)} %broadcast_in_dim.112), calls=%async_computation.2 | async-start | bytes 131072 | tf_op jit(solution)/shard_map/all_to_all | solution.py:218
  50.3 0.0 copy-start
  50.3 0.0 copy-start.2
  50.3 0.0 copy-start.5
  50.4 1.1 %copy-done.5 = f32[64,1024]{1,0:T(8,128)S(1)} copy-done((f32[64,1024]{1,0:T(8,128)S(1)}, f32[64,1024]{1,0:T(8,128)}, u32[]{:S(2)}) %copy-start.5) | copy-done | bytes 262168
  51.4 3.0 %shard_map.113.leaf_ref = f32[64,1024]{1,0:T(8,128)S(1)} custom-call(f32[1]{0:T(128)S(6)} %copy.49.signal_ref, f32[64,1]{1,0:T(8,128)S(1)} %copy.41.rate_ref, bf16[192,1024]{1,0:T(8,128)(2,1)S(1)} %pad_maximum_fusion.own_ref.other_ref, bf16[192,1024]{1,0:T(8,128)(2,1)} %collective-permute-done.1.other_ref, f32[64,1024]{1,0:T(8,128)S(1)} %copy-done.5), custom_call_target="tpu_custom_call" | custom-call | flops 1610612736 | bytes 1048576 | tf_op jit(solution)/shard_map/pallas_call | solution.py:71
  54.5 0.0 copy-start.3
  54.5 0.9 %shard_map.114 = (f32[64,1024]{1,0:T(8,128)S(1)}, f32[16,1,256]{2,1,0:T(1,128)S(1)}) custom-call(s32[1]{0:T(128)} %bitcast.place_ref, f32[1]{0:T(128)S(6)} %copy.50.noise_ref, bf16[4,32,128]{2,1,0:T(8,128)(2,1)S(1)} %multiply_convert_fusion.near_ref, bf16[4,32,128]{2,1,0:T(8,128)(2,1)S(1)} %collective-permute-done.near_other_ref, ...), custom_call_target="tpu_custom_call" | custom-call | flops 134217728 | bytes 3293192 | tf_op jit(solution)/shard_map/pallas_call | solution.py:165
  55.4 9.6 %all_to_all.25 = f32[16,1,256]{2,1,0:T(1,128)S(1)} all-to-all(f32[16,1,256]{2,1,0:T(1,128)S(1)} %get-tuple-element.9), channel_id=1, replica_groups={{480,448,416,384,352,320,288,256,224,192,160,128,96,64,32,0},{481,449,4..., dimensions={0} | all-to-all | bytes 32768 | tf_op jit(solution)/shard_map/all_to_all | solution.py:226
  65.1 15.9 %all_to_all.26.stats_ref = f32[32,1,256]{2,1,0:T(1,128)S(1)} all-to-all(f32[32,1,256]{2,1,0:T(1,128)S(1)} %broadcast_in_dim.113), channel_id=1, replica_groups={{24,16,31,17,30,18,29,19,28,20,27,21,26,22,25,23,8,0,15,1,14,2,13,3,12,..., dimensions={0} | all-to-all | bytes 65536 | tf_op jit(solution)/shard_map/all_to_all | solution.py:228
  81.0 1.3 %shard_map.115 = (f32[64,1024]{1,0:T(8,128)}, f32[64,1024]{1,0:T(8,128)}, f32[64,1024]{1,0:T(8,128)}) custom-call(f32[32,1,256]{2,1,0:T(1,128)S(1)} %all_to_all.26.stats_ref, f32[64,1024]{1,0:T(8,128)S(1)} %copy-done.3, f32[64,1024]{1,0:T(8,128)S(1)} %copy-done.2, f32[64,1024]{1,0:T(8,128)S(1)} %copy-done.1, f32[64,1024]{1,0:T(8,128)S(1)} %get-tuple-element.10.image_ref), custom_call_target="tpu_custom_call" | custom-call | bytes 1867776 | tf_op jit(solution)/shard_map/pallas_call | solution.py:165
  (29 shorter events, 0.3 us)
Async XLA Ops:
  0.8 16.7 %copy-start.1 = (f32[64,1024]{1,0:T(8,128)S(1)}, f32[64,1024]{1,0:T(8,128)}, u32[]{:S(2)}) copy-start(f32[64,1024]{1,0:T(8,128)} %direction_ref.3) | copy-start | bytes 786436
  0.8 16.8 %copy-start.6 = (bf16[64,1024]{1,0:T(8,128)(2,1)S(1)}, bf16[64,1024]{1,0:T(8,128)(2,1)}, u32[]{:S(2)}) copy-start(bf16[64,1024]{1,0:T(8,128)(2,1)} %param.9) | copy-start | bytes 393220
  3.1 16.9 %copy-start.8 = (f32[64]{0:T(128)S(1)}, f32[64]{0:T(128)}, u32[]{:S(2)}) copy-start(f32[64]{0:T(128)} %param.10) | copy-start | bytes 772
  4.2 19.8 %all-to-all-start = ((bf16[32,40,128]{2,1,0:T(8,128)(2,1)}), bf16[32,40,128]{2,1,0:T(8,128)(2,1)S(1)}, u32[]{:S(2)}, u32[]{:S(2)}) async-start(bf16[32,40,128]{2,1,0:T(8,128)(2,1)} %pad_maximum_fusion.1), calls=%async_computation | async-start | bytes 655360 | tf_op jit(solution)/shard_map/all_to_all | solution.py:198
  17.7 32.7 %collective-permute-start.1 = (bf16[192,1024]{1,0:T(8,128)(2,1)S(1)}, bf16[192,1024]{1,0:T(8,128)(2,1)}, u32[]{:S(2)}, u32[]{:S(2)}) collective-permute-start(bf16[192,1024]{1,0:T(8,128)(2,1)S(1)} %pad_maximum_fusion.own_ref.other_ref), channel_id=1, source_target_pairs={{0,16},{16,0},{1,17},{17,1},{2,18},{18,2},{3,19},{19,3},{4,20},{20... | collective-permute-start | bytes 1179656 | tf_op jit(solution)/shard_map/ppermute | solution.py:201
  21.4 2.0 %copy-start.7 = (f32[8,128]{1,0:T(8,128)S(1)}, f32[8,128]{1,0:T(8,128)}, u32[]{:S(2)}) copy-start(f32[8,128]{1,0:T(8,128)} %param.14) | copy-start | bytes 12292
  23.4 19.7 %copy-start.4 = (f32[64,1024]{1,0:T(8,128)}, f32[64,1024]{1,0:T(8,128)S(1)}, u32[]{:S(2)}) copy-start(f32[64,1024]{1,0:T(8,128)S(1)} %shard_map.112.refs_0_) | copy-start | bytes 786436
  24.8 17.5 %all-to-all-start.1 = ((bf16[16,2,128]{2,1,0:T(2,128)(2,1)}), bf16[16,2,128]{2,1,0:T(2,128)(2,1)S(1)}, u32[]{:S(2)}, u32[]{:S(2)}) async-start(bf16[16,2,128]{2,1,0:T(2,128)(2,1)} %copy.42), calls=%async_computation.1 | async-start | bytes 16384 | tf_op jit(solution)/shard_map/all_to_all | solution.py:209
  39.9 14.6 %collective-permute-start = (bf16[4,32,128]{2,1,0:T(8,128)(2,1)S(1)}, bf16[4,32,128]{2,1,0:T(8,128)(2,1)S(1)}, u32[]{:S(2)}, u32[]{:S(2)}) collective-permute-start(bf16[4,32,128]{2,1,0:T(8,128)(2,1)S(1)} %multiply_convert_fusion.near_ref), channel_id=1, source_target_pairs={{0,16},{16,0},{1,17},{17,1},{2,18},{18,2},{3,19},{19,3},{4,20},{20... | collective-permute-start | bytes 98312 | tf_op jit(solution)/shard_map/ppermute | solution.py:214
  43.1 11.4 %all-to-all-start.2 = ((bf16[32,8,128]{2,1,0:T(8,128)(2,1)}), bf16[32,8,128]{2,1,0:T(8,128)(2,1)S(1)}, u32[]{:S(2)}, u32[]{:S(2)}) async-start(bf16[32,8,128]{2,1,0:T(8,128)(2,1)} %broadcast_in_dim.112), calls=%async_computation.2 | async-start | bytes 131072 | tf_op jit(solution)/shard_map/all_to_all | solution.py:218
  50.3 4.2 %copy-start = (bf16[8,1024,128]{2,1,0:T(8,128)(2,1)S(1)}, bf16[8,1024,128]{2,1,0:T(8,128)(2,1)}, u32[]{:S(2)}) copy-start(bf16[8,1024,128]{2,1,0:T(8,128)(2,1)} %factors_ref.1) | copy-start | bytes 6291460
  50.3 4.2 %copy-start.2 = (f32[64,1024]{1,0:T(8,128)S(1)}, f32[64,1024]{1,0:T(8,128)}, u32[]{:S(2)}) copy-start(f32[64,1024]{1,0:T(8,128)} %residual_ref.3) | copy-start | bytes 786436
  50.3 1.1 %copy-start.5 = (f32[64,1024]{1,0:T(8,128)S(1)}, f32[64,1024]{1,0:T(8,128)}, u32[]{:S(2)}) copy-start(f32[64,1024]{1,0:T(8,128)} %copy-done.4) | copy-start | bytes 786436
  54.5 26.5 %copy-start.3 = (f32[64,1024]{1,0:T(8,128)S(1)}, f32[64,1024]{1,0:T(8,128)}, u32[]{:S(2)}) copy-start(f32[64,1024]{1,0:T(8,128)} %solution_ref.1) | copy-start | bytes 786436
